TPU v7x, 128 devices: a whole 4x4x4 slice. The times are simulated.
128 devices in a mesh: dp: 8 (over x_hi, y), tp: 16 (over x_lo, z, core).
Axes of the slice: x: 4 (x_hi: 2, x_lo: 2; x = x_hi * 2 + x_lo), y: 4, z: 4, core: 2. Of those that a mesh axis runs over, the one named last changes fastest.
Arguments:
- embedded: bfloat16 [2560, 4096], P(('dp', 'tp')), may hold values from -6 to 6
- upstream: bfloat16 [2560, 4096], P(('dp', 'tp')), may hold values from -6 to 6
- suffix_mask: int32 [2560], P(('dp', 'tp')), may hold values 0 or 1
- gain_attn: float32 [4096], replicated, may hold values from 0.1 to 1.9
- gain_ffn: float32 [4096], replicated, may hold values from 0.1 to 1.9
- w_query: bfloat16 [4096, 4096], P('dp', 'tp'), may hold values from -0.09375 to 0.09375
- w_keyval: bfloat16 [4096, 2048], P('dp', 'tp'), may hold values from -0.09375 to 0.09375
- w_out: bfloat16 [4096, 4096], P('tp', 'dp'), may hold values from -0.09375 to 0.09375
- w_gate: bfloat16 [4096, 14336], P('dp', 'tp'), may hold values from -0.09375 to 0.09375
- w_up: bfloat16 [4096, 14336], P('dp', 'tp'), may hold values from -0.09375 to 0.09375
- w_down: bfloat16 [14336, 4096], P('tp', 'dp'), may hold values from -0.046875 to 0.046875
Outputs:
- embed_grad: bfloat16 [2560, 4096], P(('dp', 'tp'))
All inputs are finite; a program needn't handle non-finite values. No bound on the sum of `suffix_mask` on one device may be relied on, other than what follows from the above.
Results may differ from a plain program's by a relative error of at most 0.03.
Values may be sent and summed in bfloat16 or wider, within the bound.
A program may use at most 128 MiB of HBM per device.

v0:
```python
import jax
import jax.numpy as jnp
from jax import lax
from jax.sharding import PartitionSpec as P

HD = 128
SEQ = 40


def swapped(value, axis, stride):
    mask = 2**stride
    pairs = [(source, source ^ mask) for source in range(lax.axis_size(axis))]
    return lax.ppermute(value, axis, pairs)


def rms_norm(inputs, gain):
    scale = lax.rsqrt(jnp.mean(inputs * inputs, axis=-1, keepdims=True) + 1e-05)
    return (inputs * scale * gain).astype(jnp.bfloat16)


def norm_back(upper, inputs, gain):
    scaled = upper * gain
    scale = lax.rsqrt(jnp.mean(inputs * inputs, axis=-1, keepdims=True) + 1e-05)
    return scale * scaled - inputs * scale**3 * jnp.mean(scaled * inputs, axis=-1, keepdims=True)


def rotate(vectors, sign, head_dim, seq_len):
    half = head_dim // 2
    freqs = 500000.0 ** (-jnp.arange(half, dtype=jnp.float32) * 2.0 / head_dim)
    angles = jnp.arange(seq_len, dtype=jnp.float32)[:, None] * freqs[None, :]
    cosine = jnp.cos(angles)[:, None, :]
    sine = sign * jnp.sin(angles)[:, None, :]
    first = vectors[..., :half]
    second = vectors[..., half:]
    return jnp.concatenate(
        [first * cosine - second * sine, second * cosine + first * sine], axis=-1
    )


def spread(rows):
    return lax.all_gather(rows, "tp", axis=0, tiled=True)


def reduce_rows(term_fn, rows):
    return lax.psum_scatter(
        term_fn(jnp.int32(0), rows * lax.axis_size("tp")).astype(jnp.bfloat16),
        "tp",
        scatter_dimension=0,
        tiled=True,
    ).astype(jnp.float32)


def times_transposed(left, right):
    return lax.dot_general(
        left, right, (((1,), (1,)), ((), ())), preferred_element_type=jnp.float32
    )


def per_device(
    embedded,
    upstream,
    suffix_mask,
    gain_attn,
    gain_ffn,
    w_query,
    w_keyval,
    w_out,
    w_gate,
    w_up,
    w_down,
):
    f32 = jnp.float32
    local_rows = embedded.shape[0]
    head_dim = HD
    seq_len = SEQ
    scale = 1.0 / head_dim**0.5
    full_query, full_keyval, full_out, full_gate, full_up, full_down = (
        lax.all_gather(w_query, "dp", axis=0, tiled=True),
        lax.all_gather(w_keyval, "dp", axis=0, tiled=True),
        lax.all_gather(w_out, "dp", axis=1, tiled=True),
        lax.all_gather(w_gate, "dp", axis=0, tiled=True),
        lax.all_gather(w_up, "dp", axis=0, tiled=True),
        lax.all_gather(w_down, "dp", axis=1, tiled=True),
    )
    inputs = embedded.astype(f32)
    normed_all = spread(rms_norm(inputs, gain_attn))
    group_rows = normed_all.shape[0]
    cands = group_rows // seq_len
    local_heads = full_query.shape[1] // head_dim
    query = jnp.dot(normed_all, full_query, preferred_element_type=f32).reshape(
        cands, seq_len, local_heads, head_dim
    )
    query = rotate(query, 1.0, head_dim, seq_len).astype(jnp.bfloat16)
    columns = jnp.dot(normed_all, full_keyval, preferred_element_type=f32)
    parity = lax.axis_index("tp") % 2
    rotated = rotate(columns.reshape(cands, seq_len, 1, head_dim), 1.0, head_dim, seq_len).reshape(
        group_rows, head_dim
    )
    own_part = jnp.where(parity == 0, rotated, columns).astype(jnp.bfloat16)
    other_part = swapped(own_part, "tp", 0)
    keys = jnp.where(parity == 0, own_part, other_part)
    values = jnp.where(parity == 0, other_part, own_part)
    keys = keys.reshape(cands, seq_len, head_dim)
    values = values.reshape(cands, seq_len, head_dim)
    scores = jnp.einsum("cshd,ctd->chst", query, keys, preferred_element_type=f32) * scale
    causal = jnp.arange(seq_len)[:, None] >= jnp.arange(seq_len)[None, :]
    scores = jnp.where(causal, scores, -1e30)
    scores = scores - jnp.max(scores, axis=-1, keepdims=True)
    expo = jnp.exp(scores)
    probs = expo / jnp.sum(expo, axis=-1, keepdims=True)
    probs_low = probs.astype(jnp.bfloat16)
    context = (
        jnp.einsum("chst,ctd->cshd", probs_low, values, preferred_element_type=f32)
        .astype(jnp.bfloat16)
        .reshape(group_rows, local_heads * head_dim)
    )

    def out_term(start, count):
        return jnp.dot(context, full_out, preferred_element_type=f32)

    middle = inputs + reduce_rows(out_term, local_rows)
    ffn_all = spread(rms_norm(middle, gain_ffn))
    gate = jnp.dot(ffn_all, full_gate, preferred_element_type=f32)
    up_proj = jnp.dot(ffn_all, full_up, preferred_element_type=f32)
    upstream_all = spread(upstream)
    grad_hidden = times_transposed(upstream_all, full_down)
    sigm = jax.nn.sigmoid(gate)
    grad_gate = (grad_hidden * up_proj * sigm * (1.0 + gate * (1.0 - sigm))).astype(jnp.bfloat16)
    grad_up = (grad_hidden * gate * sigm).astype(jnp.bfloat16)

    def ffn_term(start, count):
        return times_transposed(grad_gate, full_gate) + times_transposed(grad_up, full_up)

    grad_mid = upstream.astype(f32) + norm_back(reduce_rows(ffn_term, local_rows), middle, gain_ffn)
    grad_mid_all = spread(grad_mid.astype(jnp.bfloat16))
    grad_context = (
        times_transposed(grad_mid_all, full_out)
        .astype(jnp.bfloat16)
        .reshape(cands, seq_len, local_heads, head_dim)
    )
    grad_probs = jnp.einsum("cshd,ctd->chst", grad_context, values, preferred_element_type=f32)
    grad_scores = (
        probs * (grad_probs - jnp.sum(grad_probs * probs, axis=-1, keepdims=True)) * scale
    ).astype(jnp.bfloat16)
    grad_query = jnp.einsum("chst,ctd->cshd", grad_scores, keys, preferred_element_type=f32)
    grad_query = (
        rotate(grad_query, -1.0, head_dim, seq_len)
        .astype(jnp.bfloat16)
        .reshape(group_rows, local_heads * head_dim)
    )
    grad_keys = jnp.einsum("chst,cshd->ctd", grad_scores, query, preferred_element_type=f32)
    grad_keys = rotate(
        grad_keys.reshape(cands, seq_len, 1, head_dim), -1.0, head_dim, seq_len
    ).reshape(group_rows, head_dim)
    grad_values = jnp.einsum(
        "chst,cshd->ctd", probs_low, grad_context, preferred_element_type=f32
    ).reshape(group_rows, head_dim)
    outgoing = jnp.where(parity == 0, grad_values, grad_keys)
    incoming = swapped(outgoing.astype(jnp.bfloat16), "tp", 0).astype(outgoing.dtype)
    grad_cols = (jnp.where(parity == 0, grad_keys, grad_values) + incoming).astype(jnp.bfloat16)

    def attn_term(start, count):
        return times_transposed(grad_query, full_query) + times_transposed(grad_cols, full_keyval)

    result = grad_mid + norm_back(reduce_rows(attn_term, local_rows), inputs, gain_attn)
    return (result * suffix_mask[:, None].astype(f32)).astype(jnp.bfloat16)


def solution(mesh):
    placed = (
        P(("dp", "tp"), None),
        P(("dp", "tp"), None),
        P(("dp", "tp")),
        P(),
        P(),
        P("dp", "tp"),
        P("dp", "tp"),
        P("tp", "dp"),
        P("dp", "tp"),
        P("dp", "tp"),
        P("tp", "dp"),
    )
    return jax.shard_map(
        per_device, mesh=mesh, in_specs=placed, out_specs=P(("dp", "tp"), None), check_vma=False
    )
```

profile of v0, /device:TPU:1, one launch (start us, length us, event | category | flops | bytes accessed | tf_op | source)
XLA Modules:
  0.0 799.3 jit_solution(18011209550661774370)
XLA Ops:
  8.7 1.7 fusion.36
  13.9 36.4 %all-gather.27.cloned.1.call-done = bf16[16,20,4096]{2,1,0:T(8,128)(2,1)} async-done(((bf16[1,20,4096]{2,1,0:T(8,128)(2,1)}), bf16[16,20,4096]{2,1,0:T(8,128)(2,1)}) %all-gather.27.cloned.1.call-update) | async-done | bytes 2621456 | tf_op jit(solution)/shard_map/all_gather | solution.py:41
  50.3 2.8 reshape.143
  53.1 43.9 %all-gather.15.cloned.1.call-done = bf16[4096,128]{1,0:T(8,128)(2,1)} async-done(((bf16[512,128]{1,0:T(8,128)(2,1)}), bf16[4096,128]{1,0:T(8,128)(2,1)}) %all-gather.15.cloned.1.call-update) | async-done | bytes 1048592 | tf_op jit(solution)/shard_map/all_gather | solution.py:79
  97.0 2.1 fusion.70
  99.3 2.2 collective-permute-start
  101.5 51.6 %all-gather.17.cloned.1.call-done = bf16[4096,256]{1,0:T(8,128)(2,1)} async-done(((bf16[512,256]{1,0:T(8,128)(2,1)}), bf16[4096,256]{1,0:T(8,128)(2,1)}) %all-gather.17.cloned.1.call-update) | async-done | bytes 2097168 | tf_op jit(solution)/shard_map/all_gather | solution.py:78
  153.1 2.4 fusion.71
  156.3 1.2 fusion.69
  158.3 49.1 %all-gather.19.cloned.1.call-done = bf16[256,4096]{1,0:T(8,128)(2,1)} async-done(((bf16[256,512]{1,0:T(8,128)(2,1)}), bf16[256,4096]{1,0:T(8,128)(2,1)}) %all-gather.19.cloned.1.call-update) | async-done | bytes 2097168 | tf_op jit(solution)/shard_map/all_gather | solution.py:80
  207.4 2.4 convolution_convert_fusion
  209.9 43.8 %fusion = bf16[24,4096]{1,0:T(8,128)(2,1)S(1)} fusion(bf16[320,4096]{1,0:T(8,128)(2,1)S(1)} %convolution_convert_fusion), kind=kCustom, calls=%all-reduce-scatter | all-reduce-scatter fusion | flops 1572865 | bytes 2818560
  253.7 2.5 collective-permute-start.2
  256.2 1.3 collective-permute-start.3
  257.5 5.5 collective-permute-start.4
  263.0 1.2 dynamic-slice.8
  265.8 1.1 concatenate.18
  271.0 2.9 reshape.145
  273.8 32.3 %all-gather.31.cloned.1.call-done = bf16[16,20,4096]{2,1,0:T(8,128)(2,1)} async-done(((bf16[1,20,4096]{2,1,0:T(8,128)(2,1)}), bf16[16,20,4096]{2,1,0:T(8,128)(2,1)}) %all-gather.31.cloned.1.call-update) | async-done | bytes 2621456 | tf_op jit(solution)/shard_map/all_gather | solution.py:41
  306.1 4.3 reshape.147
  310.4 94.7 %all-gather.25.cloned.1.call-done = bf16[4096,896]{1,0:T(8,128)(2,1)} async-done(((bf16[512,896]{1,0:T(8,128)(2,1)}), bf16[4096,896]{1,0:T(8,128)(2,1)}) %all-gather.25.cloned.1.call-update) | async-done | bytes 7340048 | tf_op jit(solution)/shard_map/all_gather | solution.py:81
  405.1 7.7 fusion.73
  412.9 95.6 %all-gather.21.cloned.1.call-done = bf16[896,4096]{1,0:T(8,128)(2,1)} async-done(((bf16[896,512]{1,0:T(8,128)(2,1)}), bf16[896,4096]{1,0:T(8,128)(2,1)}) %all-gather.21.cloned.1.call-update) | async-done | bytes 7340048 | tf_op jit(solution)/shard_map/all_gather | solution.py:83
  508.5 7.1 fusion.72
  515.5 90.8 %all-gather.23.cloned.1.call-done = bf16[4096,896]{1,0:T(8,128)(2,1)} async-done(((bf16[512,896]{1,0:T(8,128)(2,1)}), bf16[4096,896]{1,0:T(8,128)(2,1)}) %all-gather.23.cloned.1.call-update) | async-done | bytes 7340048 | tf_op jit(solution)/shard_map/all_gather | solution.py:82
  606.3 14.4 %fusion.19 = f32[320,4096]{1,0:T(8,128)} fusion(bf16[4096,896]{1,0:T(8,128)(2,1)} %all-gather.25.cloned.1.call-done, f32[320,896]{1,0:T(8,128)} %fusion.72, bf16[320,4096]{1,0:T(8,128)(2,1)} %reshape.147, bf16[4096,896]{1,0:T(8,128)(2,1)} %all-gather.23.cloned.1.call-done, f32[320,896]{1,0:T(8,128)} %fusion.73), kind=kOutput, calls=%fused_computation.33 | convolution fusion | flops 4700487680 | bytes 24838144 | tf_op jit(solution)/shard_map/dot_general | solution.py:54
  620.7 8.2 %fusion.5 = bf16[320,4096]{1,0:T(8,128)(2,1)S(1)} fusion(f32[320,4096]{1,0:T(8,128)} %fusion.19, bf16[4096,896]{1,0:T(8,128)(2,1)} %all-gather.23.cloned.1.call-done, f32[320,896]{1,0:T(8,128)} %fusion.72, f32[320,896]{1,0:T(8,128)} %fusion.73), kind=kOutput, calls=%fused_computation.4 | convolution fusion | flops 2353152000 | bytes 17498112 | tf_op jit(solution)/shard_map/dot_general | solution.py:54
  629.0 36.7 %fusion.1 = bf16[24,4096]{1,0:T(8,128)(2,1)} fusion(bf16[320,4096]{1,0:T(8,128)(2,1)S(1)} %fusion.5), kind=kCustom, calls=%all-reduce-scatter.1 | all-reduce-scatter fusion | flops 1572865 | bytes 2818560
  665.6 1.9 collective-permute-start.5
  667.5 1.3 collective-permute-start.6
  669.8 6.1 collective-permute-start.7
  675.9 1.7 collective-permute-done.7
  677.6 2.6 concatenate.19
  680.5 1.8 convert_bitcast_fusion
  682.4 38.2 %all-gather.33.cloned.1.call-done = bf16[16,20,4096]{2,1,0:T(8,128)(2,1)} async-done(((bf16[1,20,4096]{2,1,0:T(8,128)(2,1)}), bf16[16,20,4096]{2,1,0:T(8,128)(2,1)}) %all-gather.33.cloned.1.call-update) | async-done | bytes 2621456 | tf_op jit(solution)/shard_map/all_gather | solution.py:41
  720.6 2.8 reshape.149
  723.5 3.1 convolution_convert_fusion.1
  727.6 1.2 convolution_bitcast_fusion.1
  728.9 1.8 fusion.48
  730.7 2.1 convolution_bitcast_fusion.2
  732.8 1.7 convolution_bitcast_fusion
  739.4 35.2 %fusion.2 = bf16[24,4096]{1,0:T(8,128)(2,1)} fusion(bf16[320,4096]{1,0:T(8,128)(2,1)S(1)} %fusion.6), kind=kCustom, calls=%all-reduce-scatter.2 | all-reduce-scatter fusion | flops 1572865 | bytes 2818560
  774.7 1.9 collective-permute-start.8
  776.6 1.3 collective-permute-start.9
  778.8 6.0 collective-permute-start.10
  785.5 1.3 collective-permute-done.10
  786.8 2.6 concatenate.20
  790.3 2.1 fusion.33
  (106 shorter events, 21.8 us)
Async XLA Ops:
  6.5 43.8 %all-gather.27.cloned.1.call-start = ((), (), s32[]{:S(2)}) async-start(), calls=%async_computation.6 | async-start | bytes 3342336 | tf_op jit(solution)/shard_map/all_gather | solution.py:41
  8.2 0.5 copy-start.16
  10.5 86.5 %all-gather.15.cloned.1.call-start = ((), (), s32[]{:S(2)}) async-start(), calls=%async_computation | async-start | bytes 1179648 | tf_op jit(solution)/shard_map/all_gather | solution.py:79
  11.2 141.9 %all-gather.17.cloned.1.call-start = ((), (), s32[]{:S(2)}) async-start(), calls=%async_computation.1 | async-start | bytes 2359296 | tf_op jit(solution)/shard_map/all_gather | solution.py:78
  11.9 195.4 %all-gather.19.cloned.1.call-start = ((), (), s32[]{:S(2)}) async-start(), calls=%async_computation.2 | async-start | bytes 2359296 | tf_op jit(solution)/shard_map/all_gather | solution.py:80
  12.5 258.5 %all-gather.29.cloned.1.call-start = ((), (), s32[]{:S(2)}) async-start(), calls=%async_computation.7 | async-start | bytes 3342336 | tf_op jit(solution)/shard_map/all_gather | solution.py:41
  13.1 293.0 %all-gather.31.cloned.1.call-start = ((), (), s32[]{:S(2)}) async-start(), calls=%async_computation.8 | async-start | bytes 3342336 | tf_op jit(solution)/shard_map/all_gather | solution.py:41
  13.2 144.3 %copy-start.14 = (pred[40,40]{0,1:T(8,128)(4,1)}, pred[40,40]{0,1:T(8,128)(4,1)S(1)}, u32[]{:S(2)}) copy-start(pred[40,40]{0,1:T(8,128)(4,1)S(1)} %iota_compare_fusion) | copy-start | bytes 4804
  13.9 142.2 %copy-start.4 = (f32[40,64]{1,0:T(8,128)}, f32[40,64]{1,0:T(8,128)S(1)}, u32[]{:S(2)}) copy-start(f32[40,64]{1,0:T(8,128)S(1)} %get-tuple-element.21) | copy-start | bytes 30724
  99.3 56.9 %collective-permute-start = (bf16[320,128]{1,0:T(8,128)(2,1)S(1)}, bf16[320,128]{1,0:T(8,128)(2,1)S(1)}, u32[]{:S(2)}, u32[]{:S(2)}) collective-permute-start(bf16[320,128]{1,0:T(8,128)(2,1)S(1)} %fusion.45), channel_id=1, source_target_pairs={{0,1},{1,0},{2,3},{3,2},{4,5},{5,4},{6,7},{7,6},{8,9},{9,8},{10,11... | collective-permute-start | bytes 245768 | tf_op jit(solution)/shard_map/ppermute | solution.py:13
  156.2 51.2 %copy-start.9 = (bf16[8,40,2,64]{3,1,2,0:T(8,128)(2,1)}, bf16[8,40,2,64]{3,1,2,0:T(8,128)(2,1)S(1)}, u32[]{:S(2)}) copy-start(bf16[8,40,2,64]{3,1,2,0:T(8,128)(2,1)S(1)} %get-tuple-element.5) | copy-start | bytes 245764
  156.3 51.2 %copy-start.11 = (bf16[8,40,2,64]{3,1,2,0:T(8,128)(2,1)}, bf16[8,40,2,64]{3,1,2,0:T(8,128)(2,1)S(1)}, u32[]{:S(2)}) copy-start(bf16[8,40,2,64]{3,1,2,0:T(8,128)(2,1)S(1)} %get-tuple-element.6) | copy-start | bytes 245764
  156.3 1.2 copy-start.6
  156.3 1.2 copy-start.13
  157.5 52.4 %copy-start.18 = (f32[8,2,40]{2,1,0:T(2,128)}, f32[8,2,40]{2,1,0:T(2,128)S(1)}, u32[]{:S(2)}) copy-start(f32[8,2,40]{2,1,0:T(2,128)S(1)} %get-tuple-element.24) | copy-start | bytes 7684
  209.9 57.1 %copy-start = (bf16[20,4096]{1,0:T(8,128)(2,1)S(1)}, bf16[20,4096]{1,0:T(8,128)(2,1)}, u32[]{:S(2)}) copy-start(bf16[20,4096]{1,0:T(8,128)(2,1)} %param.11) | copy-start | bytes 491524
  209.9 57.8 %copy-start.8 = (f32[4096]{0:T(1024)S(1)}, f32[4096]{0:T(1024)}, u32[]{:S(2)}) copy-start(f32[4096]{0:T(1024)} %param.15) | copy-start | bytes 49156
  253.7 12.1 %collective-permute-start.2 = (bf16[24,4096]{1,0:T(8,128)(2,1)S(1)}, bf16[24,4096]{1,0:T(8,128)(2,1)S(1)}, u32[]{:S(2)}, u32[]{:S(2)}) collective-permute-start(bf16[24,4096]{1,0:T(8,128)(2,1)S(1)} %fusion), channel_id=1, source_target_pairs={{0,1},{1,2},{2,3},{3,4},{4,5},{5,6},{6,7},{7,8},{8,9},{9,10},{10,1... | collective-permute-start | bytes 589832
  256.2 9.6 %collective-permute-start.3 = (bf16[24,4096]{1,0:T(8,128)(2,1)S(1)}, bf16[24,4096]{1,0:T(8,128)(2,1)S(1)}, u32[]{:S(2)}, u32[]{:S(2)}) collective-permute-start(bf16[24,4096]{1,0:T(8,128)(2,1)S(1)} %fusion), channel_id=1, source_target_pairs={{0,2},{1,3},{2,4},{3,5},{4,6},{5,7},{6,8},{7,9},{8,10},{9,11},{10,... | collective-permute-start | bytes 589832
  257.5 8.3 %collective-permute-start.4 = (bf16[12,4096]{1,0:T(8,128)(2,1)S(1)}, bf16[12,4096]{1,0:T(8,128)(2,1)S(1)}, u32[]{:S(2)}, u32[]{:S(2)}) collective-permute-start(bf16[12,4096]{1,0:T(8,128)(2,1)S(1)} %slice.40), channel_id=1, source_target_pairs={{0,3},{1,4},{2,5},{3,6},{4,7},{5,8},{6,9},{7,10},{8,11},{9,12},{10... | collective-permute-start | bytes 294920
  267.7 3.3 copy-start.15
  268.5 136.6 %all-gather.25.cloned.1.call-start = ((), (), s32[]{:S(2)}) async-start(), calls=%async_computation.5 | async-start | bytes 8257536 | tf_op jit(solution)/shard_map/all_gather | solution.py:81
  269.2 239.2 %all-gather.21.cloned.1.call-start = ((), (), s32[]{:S(2)}) async-start(), calls=%async_computation.3 | async-start | bytes 8257536 | tf_op jit(solution)/shard_map/all_gather | solution.py:83
  270.0 336.3 %all-gather.23.cloned.1.call-start = ((), (), s32[]{:S(2)}) async-start(), calls=%async_computation.4 | async-start | bytes 8257536 | tf_op jit(solution)/shard_map/all_gather | solution.py:82
  270.7 449.9 %all-gather.33.cloned.1.call-start = ((), (), s32[]{:S(2)}) async-start(), calls=%async_computation.9 | async-start | bytes 3342336 | tf_op jit(solution)/shard_map/all_gather | solution.py:41
  665.6 12.0 %collective-permute-start.5 = (bf16[24,4096]{1,0:T(8,128)(2,1)}, bf16[24,4096]{1,0:T(8,128)(2,1)S(1)}, u32[]{:S(2)}, u32[]{:S(2)}) collective-permute-start(bf16[24,4096]{1,0:T(8,128)(2,1)} %fusion.1), channel_id=1, source_target_pairs={{0,1},{1,2},{2,3},{3,4},{4,5},{5,6},{6,7},{7,8},{8,9},{9,10},{10,1... | collective-permute-start | bytes 589832
  667.5 10.1 %collective-permute-start.6 = (bf16[24,4096]{1,0:T(8,128)(2,1)}, bf16[24,4096]{1,0:T(8,128)(2,1)S(1)}, u32[]{:S(2)}, u32[]{:S(2)}) collective-permute-start(bf16[24,4096]{1,0:T(8,128)(2,1)} %fusion.1), channel_id=1, source_target_pairs={{0,2},{1,3},{2,4},{3,5},{4,6},{5,7},{6,8},{7,9},{8,10},{9,11},{10,... | collective-permute-start | bytes 589832
  669.8 7.8 collective-permute-start.7
  680.2 2.2 copy-start.2
  680.5 1.9 copy-start.17
  726.6 4.1 copy-start.10
  726.6 4.1 copy-start.12
  726.6 4.1 copy-start.19
  728.8 1.9 copy-start.7
  728.8 5.7 copy-start.5
  732.8 4.5 copy-start.3
  735.8 2.4 collective-permute-start.1
  737.3 1.2 copy-start.1
  774.7 12.1 %collective-permute-start.8 = (bf16[24,4096]{1,0:T(8,128)(2,1)}, bf16[24,4096]{1,0:T(8,128)(2,1)S(1)}, u32[]{:S(2)}, u32[]{:S(2)}) collective-permute-start(bf16[24,4096]{1,0:T(8,128)(2,1)} %fusion.2), channel_id=1, source_target_pairs={{0,1},{1,2},{2,3},{3,4},{4,5},{5,6},{6,7},{7,8},{8,9},{9,10},{10,1... | collective-permute-start | bytes 589832
  776.6 10.2 %collective-permute-start.9 = (bf16[24,4096]{1,0:T(8,128)(2,1)}, bf16[24,4096]{1,0:T(8,128)(2,1)S(1)}, u32[]{:S(2)}, u32[]{:S(2)}) collective-permute-start(bf16[24,4096]{1,0:T(8,128)(2,1)} %fusion.2), channel_id=1, source_target_pairs={{0,2},{1,3},{2,4},{3,5},{4,6},{5,7},{6,8},{7,9},{8,10},{9,11},{10,... | collective-permute-start | bytes 589832
  778.8 7.9 collective-permute-start.10
Sparse Core Ops, SparseCore 0:
  10.6 39.6 all-gather.26
  52.6 44.2 all-gather.14
  99.4 53.7 all-gather.16
  155.2 52.2 all-gather.18
  208.9 37.3 all-gather.28
  268.6 37.4 all-gather.30
  308.4 96.6 all-gather.24
  407.3 101.1 all-gather.20
  510.8 95.4 all-gather.22
  682.5 38.0 all-gather.32
where the time goes:
time: 806 us; the launch traced here: 799 us
  waiting for transfers between devices  541 us (67%)
  blocking collectives  116 us (14%)
  matrix products  57.9 us (7%)
  starting transfers between devices  30.8 us (4%)
  local copies, waits for them, and re-layouts  25.1 us (3%)
  between operations  14.7 us (2%)
  other arithmetic  14 us (2%)
    unnamed x3, blocking collectives  116 us
    all_gather x4, waiting for transfers between devices, spread(): return lax.all_gather(rows, 'tp', axis=0, tiled=True)  107 us
    all_gather x1, waiting for transfers between devices, per_device(): lax.all_gather(w_down, 'dp', axis=1, tiled=True)  95.6 us
    all_gather x1, waiting for transfers between devices, per_device(): lax.all_gather(w_gate, 'dp', axis=0, tiled=True)  94.7 us
    all_gather x1, waiting for transfers between devices, per_device(): lax.all_gather(w_up, 'dp', axis=0, tiled=True)  90.8 us
    all_gather x1, waiting for transfers between devices, per_device(): lax.all_gather(w_query, 'dp', axis=0, tiled=True)  51.6 us
    all_gather x1, waiting for transfers between devices, per_device(): lax.all_gather(w_out, 'dp', axis=1, tiled=True)  49.1 us
    all_gather x1, waiting for transfers between devices, per_device(): lax.all_gather(w_keyval, 'dp', axis=0, tiled=True)  43.9 us
  transfers between devices with their start and end apart: 21, of which 12 were waited for; matrix products, arithmetic and copies ran while one was open for 11% of the time, Pallas kernels for 0%

commit v1 on v0

v1 whole, which is shorter than its diff:
```python
import functools

import jax
import jax.numpy as jnp
import numpy as np
from jax import lax
from jax.experimental import pallas as pl
from jax.experimental.pallas import tpu as pltpu
from jax.sharding import PartitionSpec as P

MESH = pl.DeviceIdType.MESH
D = 4096
HALF = 2048
QUART = 1024
FFB = 896
HD = 128
SEQ = 40
ROWS = 48
CROWS = 24
LIVE = 20
GROUP = 4 * ROWS
OWN = 8 * ROWS
F32 = jnp.float32
BF16 = jnp.bfloat16


def dot_nn(left, right):
    return jnp.dot(left, right, preferred_element_type=F32)


def dot_nt(left, right):
    return lax.dot_general(left, right, (((1,), (1,)), ((), ())), preferred_element_type=F32)


def dot_tn(left, right):
    return lax.dot_general(left, right, (((0,), (0,)), ((), ())), preferred_element_type=F32)


def device_of(x, y, z, core):
    return ((x // 2) * 4 + y, (x % 2) * 8 + z * 2 + core)


def remote(src, dst, send_sem, recv_sem, device):
    return pltpu.make_async_remote_copy(
        src_ref=src, dst_ref=dst, send_sem=send_sem, recv_sem=recv_sem, device_id=device, device_id_type=MESH
    )


def arrived(dst, sem):
    pltpu.make_async_copy(dst, dst, sem).wait()


def kernel(
    emb, ups, gain_a, gain_f, cos_ref, sin_ref, mask_ref,
    w_q, w_kv, w_o, w_g, w_u, w_d,
    out_ref,
    xbuf, ubuf, mbuf, gbuf, fin, st_src, st_dst,
    wqkv, wo, wd, wg, wu,
    acts, part, rs_a, rs_b, rs_c, rs_d,
    qkv_own, qkv_send, qkv_recv, qb, kb, vb, probs, ctx, dctx_own, dctx_send, dctx_recv, dqkv,
    ffn_own, ffn_send, ffn_recv, ggu,
    ex_s, ex_r, st_s, st_r, x_s, x_r, y_s, y_r, ag_s, ag_r, rs_s, rs_r, cx_s, cx_r,
):
    dp, tp = lax.axis_index("dp"), lax.axis_index("tp")
    x_hi, y = dp // 4, dp % 4
    x_lo, z, core = tp // 8, (tp // 2) % 4, tp % 2
    x = x_hi * 2 + x_lo
    other = 1 - core
    partner = device_of(x, y, z, other)
    across_same = device_of((x + 2) % 4, y, z, core)
    across_other = device_of((x + 2) % 4, y, z, other)
    y_up = device_of(x, (y + 1) % 4, z, core)
    y_dn = device_of(x, (y + 3) % 4, z, core)

    def ring(is_x, step):
        return device_of((x + step * is_x) % 4, y, (z + step * (1 - is_x)) % 4, core)

    r1_up, r1_dn = ring(core, 1), ring(core, 3)
    r2_up, r2_dn = ring(other, 1), ring(other, 3)
    p1 = core * x + other * z
    p2 = core * z + other * x

    def slot(a, b):
        return (a % 4) * (1 + 3 * core) + (b % 4) * (4 - 3 * core)

    me = slot(p1, p2)
    diag = core == x_hi
    col0 = pl.multiple_of(core * HALF, HALF)
    col1 = pl.multiple_of(other * HALF, HALF)
    row0 = pl.multiple_of(core * CROWS, CROWS)

    barrier = pltpu.get_barrier_semaphore()
    friends = (partner, across_same, across_other, y_up, y_dn, r1_up, r1_dn, r2_up, r2_dn)
    for friend in friends:
        pl.semaphore_signal(barrier, inc=1, device_id=friend, device_id_type=MESH)
    pl.semaphore_wait(barrier, len(friends))

    ex = []
    for i, (src, dst) in enumerate(((emb, xbuf), (ups, ubuf))):
        copy = remote(src.at[:, pl.ds(col1, HALF)], dst.at[pl.ds(row0, CROWS)], ex_s.at[i], ex_r.at[i], partner)
        copy.start()
        ex.append(copy)

    yrow = pl.multiple_of(y * 512, 512)
    kvcol = pl.multiple_of(256 + core * HD, HD)
    own_parts = (
        (w_q, wqkv.at[pl.ds(yrow, 512), pl.ds(0, 256)]),
        (w_o, wo.at[:, pl.ds(yrow, 512)]),
        (w_d, wd.at[:, pl.ds(yrow, 512)]),
        (w_g, wg.at[pl.ds(yrow, 512)]),
        (w_u, wu.at[pl.ds(yrow, 512)]),
    )
    kv_part = wqkv.at[pl.ds(yrow, 512), pl.ds(kvcol, HD)]
    k_part = wqkv.at[pl.ds(yrow, 512), pl.ds(256, HD)]
    v_part = wqkv.at[pl.ds(yrow, 512), pl.ds(256 + HD, HD)]

    def swap_local(i):
        @pl.when(diag)
        def _():
            pltpu.make_async_copy(*own_parts[i], x_r.at[i]).start()

    def swap_remote(i):
        src, dst = own_parts[i]

        @pl.when(jnp.logical_not(diag))
        def _():
            remote(src, dst, x_s.at[i], x_r.at[i], across_other).start()

    def swap_wait(i):
        arrived(own_parts[i][1], x_r.at[i])

    def swap_drain(i):
        src, dst = own_parts[i]

        @pl.when(jnp.logical_not(diag))
        def _():
            remote(src, dst, x_s.at[i], x_r.at[i], across_other).wait_send()

    def kv_start():
        @pl.when(diag)
        def _():
            pltpu.make_async_copy(w_kv, kv_part, x_r.at[5 + core]).start()
            remote(w_kv, kv_part, x_s.at[6], x_r.at[5 + core], across_same).start()

        @pl.when(jnp.logical_not(diag))
        def _():
            remote(w_kv, kv_part, x_s.at[5], x_r.at[5 + core], partner).start()
            remote(w_kv, kv_part, x_s.at[6], x_r.at[5 + core], across_other).start()

    def kv_wait():
        arrived(k_part, x_r.at[5])
        arrived(v_part, x_r.at[6])

    def kv_drain():
        @pl.when(jnp.logical_not(diag))
        def _():
            remote(w_kv, kv_part, x_s.at[5], x_r.at[5 + core], partner).wait_send()

        remote(w_kv, kv_part, x_s.at[6], x_r.at[5 + core], across_same).wait_send()

    def piece(i, at, half=None):
        base = pl.multiple_of((at % 4) * 512, 512)
        if i in (1, 2):
            buf, rows = (wo, 256) if i == 1 else (wd, FFB)
            if half is None:
                return buf.at[:, pl.ds(base, 512)]
            return buf.at[pl.ds(half * rows // 2, rows // 2), pl.ds(base, 512)]
        buf = {0: wqkv, 3: wg, 4: wu}[i]
        if half is None:
            return buf.at[pl.ds(base, 512)]
        return buf.at[pl.ds(base + half * 256, 256)]

    def y1_copies(i):
        ref = piece(i, y)
        return (
            remote(ref, ref, y_s.at[4 * i], y_r.at[4 * i], y_up),
            remote(ref, ref, y_s.at[4 * i + 1], y_r.at[4 * i + 1], y_dn),
        )

    def y2_copies(i):
        from_dn, from_up = piece(i, y + 3, 0), piece(i, y + 1, 1)
        return (
            remote(from_dn, from_dn, y_s.at[4 * i + 2], y_r.at[4 * i + 2], y_up),
            remote(from_up, from_up, y_s.at[4 * i + 3], y_r.at[4 * i + 3], y_dn),
        )

    def y1_start(i):
        for copy in y1_copies(i):
            copy.start()

    def y2_start(i):
        up, dn = y2_copies(i)
        arrived(piece(i, y + 3), y_r.at[4 * i])
        up.start()
        arrived(piece(i, y + 1), y_r.at[4 * i + 1])
        dn.start()

    def y_finish(i):
        arrived(piece(i, y + 2, 0), y_r.at[4 * i + 2])
        arrived(piece(i, y + 2, 1), y_r.at[4 * i + 3])

    def y_drain(i):
        for copy in (*y1_copies(i), *y2_copies(i)):
            copy.wait_send()

    def ag_copy(k, ref, n_send, n_recv, device):
        return remote(ref, ref, ag_s.at[k, n_send], ag_r.at[k, n_recv], device)

    def ag_refs(k, index):
        full = acts.at[k, index]
        return full, acts.at[k, index, :, pl.ds(0, QUART)], acts.at[k, index, :, pl.ds(QUART, QUART)]

    offs = (0, 3, 1, 2)

    def ag_get(k, name, j=0):
        mine = ag_refs(k, slot(p1 + offs[j], p2))[0]
        at = 4 + 4 * j
        if name == "a":
            return ag_copy(k, ag_refs(k, me)[0], 0, 0, r1_up)
        if name == "b":
            return ag_copy(k, ag_refs(k, me)[0], 1, 1, r1_dn)
        if name == "c":
            return ag_copy(k, ag_refs(k, slot(p1 + 3, p2))[1], 2, 2, r1_up)
        if name == "d":
            return ag_copy(k, ag_refs(k, slot(p1 + 1, p2))[2], 3, 3, r1_dn)
        if name == "up":
            return ag_copy(k, mine, at, at, r2_up)
        if name == "dn":
            return ag_copy(k, mine, at + 1, at + 1, r2_dn)
        if name == "up2":
            return ag_copy(k, ag_refs(k, slot(p1 + offs[j], p2 + 3))[1], at + 2, at + 2, r2_up)
        return ag_copy(k, ag_refs(k, slot(p1 + offs[j], p2 + 1))[2], at + 3, at + 3, r2_dn)

    def ag_start(k):
        for name in ("a", "b", "up", "dn"):
            ag_get(k, name).start()

    def ag_run(k):
        arrived(ag_refs(k, slot(p1 + 3, p2))[0], ag_r.at[k, 0])
        ag_get(k, "c").start()
        ag_get(k, "up", 1).start()
        ag_get(k, "dn", 1).start()
        arrived(ag_refs(k, slot(p1 + 1, p2))[0], ag_r.at[k, 1])
        ag_get(k, "d").start()
        ag_get(k, "up", 2).start()
        ag_get(k, "dn", 2).start()

        def through(j):
            arrived(ag_refs(k, slot(p1 + offs[j], p2 + 3))[0], ag_r.at[k, 4 + 4 * j])
            ag_get(k, "up2", j).start()
            arrived(ag_refs(k, slot(p1 + offs[j], p2 + 1))[0], ag_r.at[k, 5 + 4 * j])
            ag_get(k, "dn2", j).start()

        through(0)
        arrived(ag_refs(k, slot(p1 + 2, p2))[1], ag_r.at[k, 2])
        arrived(ag_refs(k, slot(p1 + 2, p2))[2], ag_r.at[k, 3])
        ag_get(k, "up", 3).start()
        ag_get(k, "dn", 3).start()
        for j in (1, 2, 3):
            through(j)
        for j in range(4):
            far = ag_refs(k, slot(p1 + offs[j], p2 + 2))
            arrived(far[1], ag_r.at[k, 6 + 4 * j])
            arrived(far[2], ag_r.at[k, 7 + 4 * j])
        for name in ("a", "b", "c", "d"):
            ag_get(k, name).wait_send()
        for j in range(4):
            for name in ("up", "dn", "up2", "dn2"):
                ag_get(k, name, j).wait_send()

    def rs_run(k, compute, between=None):
        def send(src, dst, n, device):
            copy = remote(src, dst, rs_s.at[k, n], rs_r.at[k, n], device)
            copy.start()
            return copy

        lo, hi = pl.ds(0, QUART), pl.ds(QUART, QUART)
        sent = []
        compute(2)
        for i in range(4):
            at = slot(p1 + i, p2 + 2)
            sent.append(send(part.at[at, :, lo], rs_a.at[k, 0, i], 2 * i, r2_up))
            sent.append(send(part.at[at, :, hi], rs_a.at[k, 1, i], 2 * i + 1, r2_dn))
        compute(1)
        compute(3)
        for i in range(4):
            at = slot(p1 + i, p2 + 1)
            arrived(rs_a.at[k, 0, i], rs_r.at[k, 2 * i])
            part[at, :, lo] = (part[at, :, lo].astype(F32) + rs_a[k, 0, i].astype(F32)).astype(BF16)
            sent.append(send(part.at[at], rs_b.at[k, 0, i], 8 + 2 * i, r2_up))
            at = slot(p1 + i, p2 + 3)
            arrived(rs_a.at[k, 1, i], rs_r.at[k, 2 * i + 1])
            part[at, :, hi] = (part[at, :, hi].astype(F32) + rs_a[k, 1, i].astype(F32)).astype(BF16)
            sent.append(send(part.at[at], rs_b.at[k, 1, i], 9 + 2 * i, r2_dn))
        compute(0)

        def add_both(i):
            at = slot(p1 + i, p2)
            arrived(rs_b.at[k, 0, i], rs_r.at[k, 8 + 2 * i])
            arrived(rs_b.at[k, 1, i], rs_r.at[k, 9 + 2 * i])
            return part[at].astype(F32) + rs_b[k, 0, i].astype(F32) + rs_b[k, 1, i].astype(F32)

        at = slot(p1 + 2, p2)
        part[at] = add_both(2).astype(BF16)
        sent.append(send(part.at[at, :, lo], rs_c.at[k, 0], 16, r1_up))
        sent.append(send(part.at[at, :, hi], rs_c.at[k, 1], 17, r1_dn))
        at = slot(p1 + 1, p2)
        part[at] = add_both(1).astype(BF16)
        arrived(rs_c.at[k, 0], rs_r.at[k, 16])
        part[at, :, lo] = (part[at, :, lo].astype(F32) + rs_c[k, 0].astype(F32)).astype(BF16)
        sent.append(send(part.at[at], rs_d.at[k, 0], 18, r1_up))
        at = slot(p1 + 3, p2)
        part[at] = add_both(3).astype(BF16)
        arrived(rs_c.at[k, 1], rs_r.at[k, 17])
        part[at, :, hi] = (part[at, :, hi].astype(F32) + rs_c[k, 1].astype(F32)).astype(BF16)
        sent.append(send(part.at[at], rs_d.at[k, 1], 19, r1_dn))
        total = add_both(0)
        arrived(rs_d.at[k, 0], rs_r.at[k, 18])
        arrived(rs_d.at[k, 1], rs_r.at[k, 19])
        total = total + rs_d[k, 0].astype(F32) + rs_d[k, 1].astype(F32)
        for copy in sent:
            copy.wait_send()
        return total

    def both_halves(i, value):
        mine = jnp.broadcast_to(jnp.sum(value, axis=-1, keepdims=True), (ROWS, HD))
        st_src[i] = mine
        copy = remote(st_src.at[i], st_dst.at[i], st_s.at[i], st_r.at[i], partner)
        copy.start()
        copy.wait()
        return (mine + st_dst[i])[:, :1] * (1.0 / D)

    def in_chip(i, src, dst):
        copy = remote(src, dst, cx_s.at[i], cx_r.at[i], partner)
        copy.start()
        return copy

    def group_rows(ref, at):
        return jnp.concatenate([ref[slot(p1 + i, p2 + at)] for i in range(4)], axis=0)

    def halves_matmul(k, weights_fn, send_ref, own_ref):
        def step(i, carry):
            rows = acts[k, pl.ds(8 * other + 4 * i, 4)].reshape(GROUP, HALF)
            send_ref[i] = weights_fn(rows).astype(BF16)
            return carry

        lax.fori_loop(0, 2, step, 0)

        def finish():
            def own_step(i, carry):
                rows = acts[k, pl.ds(8 * core + 4 * i, 4)].reshape(GROUP, HALF)
                own_ref[i] = weights_fn(rows)
                return carry

            lax.fori_loop(0, 2, own_step, 0)

        return finish

    def rope(value, sign):
        return value * cos_ref[...] + sign * pltpu.roll(value, HD // 2, 1) * sin_ref[...]

    def ready_y1(pieces):
        for i in pieces:
            if i == 0:
                kv_wait()
            swap_wait(i)
            y1_start(i)

    def when_diag(fn):
        pl.when(diag)(fn)

    def when_off(fn):
        pl.when(jnp.logical_not(diag))(fn)

    swap_remote(0)
    kv_start()
    swap_remote(1)
    for i in range(5):
        swap_local(i)
    gain_attn = gain_a[:, pl.ds(col0, HALF)]
    gain_ffn = gain_f[:, pl.ds(col0, HALF)]
    xbuf[pl.ds(row0, CROWS)] = emb[:, pl.ds(col0, HALF)]
    ubuf[pl.ds(row0, CROWS)] = ups[:, pl.ds(col0, HALF)]
    ex[0].wait()
    inputs = xbuf[...]
    r_attn = lax.rsqrt(both_halves(0, inputs * inputs) + 1e-05)
    acts[0, me] = (inputs * r_attn * gain_attn).astype(BF16)
    ag_start(0)
    when_diag(lambda: ready_y1((0, 1, 2)))
    ex[1].wait()
    acts[1, me] = ubuf[...].astype(BF16)
    when_off(lambda: ready_y1((0, 1)))
    ag_run(0)
    swap_remote(2)
    y2_start(0)
    y2_start(1)
    ag_start(1)
    when_diag(lambda: ready_y1((3,)))
    y_finish(0)

    finish = halves_matmul(0, lambda rows: dot_nn(rows, wqkv[...]), qkv_send, qkv_own)
    copy = in_chip(0, qkv_send, qkv_recv)
    finish()
    copy.wait()
    scale = 1.0 / HD**0.5

    def attend(g, carry):
        total = qkv_own[g] + qkv_recv[g].astype(F32)
        keys = rope(total[:, 256:384], 1.0).astype(BF16)
        values = total[:, 384:].astype(BF16)
        kb[g] = keys
        vb[g] = values
        for h in range(2):
            cols = slice(h * HD, (h + 1) * HD)
            query = rope(total[:, cols], 1.0).astype(BF16)
            qb[g, :, cols] = query
            scores = jnp.where(mask_ref[...] > 0, dot_nt(query, keys) * scale, -1e30)
            expo = jnp.exp(scores - jnp.max(scores, axis=-1, keepdims=True))
            prob = expo / jnp.sum(expo, axis=-1, keepdims=True)
            probs[g, h] = prob
            out = dot_nn(prob.astype(BF16), values).astype(BF16)
            ctx[pl.ds(8 * core + 4 * g, 4), :, cols] = out.reshape(4, ROWS, HD)
        return carry

    lax.fori_loop(0, 2, attend, 0)
    mine = pl.ds(8 * core, 8)
    copy = in_chip(1, ctx.at[mine], ctx.at[mine])
    ag_run(1)
    when_diag(lambda: ready_y1((4,)))
    when_off(lambda: ready_y1((2,)))
    swap_remote(3)
    when_diag(lambda: y2_start(2))
    y_finish(1)
    copy.wait()

    def spread_group(at, term):
        def step(n, carry):
            cols = pl.ds(pl.multiple_of(n * 512, 512), 512)
            value = term(cols).astype(BF16)
            for i in range(4):
                part[slot(p1 + i, p2 + at), :, cols] = value[i * ROWS:(i + 1) * ROWS]
            return carry

        lax.fori_loop(0, 4, step, 0)

    def out_term(at):
        rows = group_rows(ctx, at)
        spread_group(at, lambda cols: dot_nn(rows, wo[:, cols]))

    middle = inputs + rs_run(0, out_term)
    mbuf[...] = middle
    when_off(lambda: ready_y1((3,)))
    swap_remote(4)
    when_diag(lambda: y2_start(3))
    when_off(lambda: y2_start(2))
    r_ffn = lax.rsqrt(both_halves(1, middle * middle) + 1e-05)
    acts[2, me] = (middle * r_ffn * gain_ffn).astype(BF16)
    ag_start(2)
    when_diag(lambda: y2_start(4))
    ag_run(2)
    when_off(lambda: ready_y1((4,)))
    when_off(lambda: y2_start(3))

    def ffn_part(j, k, weights_fn):
        finish = halves_matmul(k, weights_fn, ffn_send.at[j], ffn_own.at[j])
        copy = in_chip(2 + j, ffn_send.at[j], ffn_recv.at[j])
        finish()
        return copy

    copies = []
    y_finish(2)
    copies.append(ffn_part(0, 1, lambda rows: dot_nt(rows, wd[...])))
    when_off(lambda: y2_start(4))
    y_finish(3)
    copies.append(ffn_part(1, 2, lambda rows: dot_nn(rows, wg[...])))
    y_finish(4)
    copies.append(ffn_part(2, 2, lambda rows: dot_nn(rows, wu[...])))
    for copy in copies:
        copy.wait()

    def gates(i, carry):
        g, rows = i // 4, pl.ds(pl.multiple_of((i % 4) * ROWS, ROWS), ROWS)
        hidden, gate, up = (ffn_own[j, g, rows] + ffn_recv[j, g, rows].astype(F32) for j in range(3))
        sigm = jax.nn.sigmoid(gate)
        lifted = hidden * sigm
        ggu[0, 8 * core + i] = (lifted * up * (1.0 + gate * (1.0 - sigm))).astype(BF16)
        ggu[1, 8 * core + i] = (lifted * gate).astype(BF16)
        return carry

    lax.fori_loop(0, 8, gates, 0)
    copies = [in_chip(5 + j, ggu.at[j, mine], ggu.at[j, mine]) for j in range(2)]
    for copy in copies:
        copy.wait()

    def ffn_term(at):
        gate_rows, up_rows = group_rows(ggu.at[0], at), group_rows(ggu.at[1], at)
        spread_group(at, lambda cols: dot_nt(gate_rows, wg[cols]) + dot_nt(up_rows, wu[cols]))

    scaled = rs_run(1, ffn_term) * gain_ffn
    middle = mbuf[...]
    mean = both_halves(2, scaled * middle)
    grad_mid = ubuf[...] + r_ffn * scaled - middle * r_ffn**3 * mean
    gbuf[...] = grad_mid
    acts[3, me] = grad_mid.astype(BF16)
    ag_start(3)
    ag_run(3)

    finish = halves_matmul(3, lambda rows: dot_nt(rows, wo[...]), dctx_send, dctx_own)
    copy = in_chip(7, dctx_send, dctx_recv)
    finish()
    copy.wait()

    def attend_back(g, carry):
        upper = (dctx_own[g] + dctx_recv[g].astype(F32)).astype(BF16)
        keys, values = kb[g], vb[g]
        here = pl.ds(8 * core + 4 * g, 4)
        grad_keys = jnp.zeros((GROUP, HD), F32)
        grad_values = jnp.zeros((GROUP, HD), F32)
        for h in range(2):
            cols = slice(h * HD, (h + 1) * HD)
            prob = probs[g, h]
            grad_probs = dot_nt(upper[:, cols], values)
            grad_scores = (
                prob * (grad_probs - jnp.sum(grad_probs * prob, axis=-1, keepdims=True)) * scale
            ).astype(BF16)
            grad_query = rope(dot_nn(grad_scores, keys), -1.0).astype(BF16)
            dqkv[here, :, cols] = grad_query.reshape(4, ROWS, HD)
            grad_keys += dot_tn(grad_scores, qb[g, :, cols])
            grad_values += dot_tn(prob.astype(BF16), upper[:, cols])
        dqkv[here, :, 256:384] = rope(grad_keys, -1.0).astype(BF16).reshape(4, ROWS, HD)
        dqkv[here, :, 384:] = grad_values.astype(BF16).reshape(4, ROWS, HD)
        return carry

    lax.fori_loop(0, 2, attend_back, 0)
    in_chip(8, dqkv.at[mine], dqkv.at[mine]).wait()

    def attn_term(at):
        rows = group_rows(dqkv, at)
        spread_group(at, lambda cols: dot_nt(rows, wqkv[cols]))

    scaled = rs_run(2, attn_term) * gain_attn
    inputs = xbuf[...]
    mean = both_halves(3, scaled * inputs)
    mbuf[...] = gbuf[...] + r_attn * scaled - inputs * r_attn**3 * mean
    row1 = pl.multiple_of(other * CROWS, CROWS)
    copy = in_chip(9, mbuf.at[pl.ds(row1, CROWS)], fin.at[:, pl.ds(col0, HALF)])
    fin[:, pl.ds(col0, HALF)] = mbuf[pl.ds(row0, CROWS)]
    for i in range(5):
        swap_drain(i)
        y_drain(i)
    kv_drain()
    copy.wait()
    out_ref[...] = fin[...]


def tables():
    place = np.arange(ROWS) % CROWS
    spot = np.minimum(place, LIVE - 1) + LIVE * (np.arange(ROWS) // CROWS)
    freqs = np.float32(500000.0) ** (-np.arange(HD // 2, dtype=np.float32) * np.float32(2.0 / HD))
    angles = spot.astype(np.float32)[:, None] * freqs[None, :]
    cosine, sine = np.cos(angles), np.sin(angles)
    cosine = np.tile(np.concatenate([cosine, cosine], axis=1), (4, 1)).astype(np.float32)
    sine = np.tile(np.concatenate([-sine, sine], axis=1), (4, 1)).astype(np.float32)
    cand = np.arange(GROUP) // ROWS
    spots, live = np.tile(spot, 4), np.tile(place < LIVE, 4)
    mask = (cand[:, None] == cand[None, :]) & live[None, :] & (spots[:, None] >= spots[None, :])
    return cosine, sine, mask.astype(np.float32)


def per_device(embedded, upstream, suffix_mask, gain_attn, gain_ffn, w_query, w_keyval, w_out, w_gate, w_up, w_down):
    pad = ((0, CROWS - LIVE), (0, 0))
    vmem = pl.BlockSpec(memory_space=pltpu.VMEM)
    hbm = pl.BlockSpec(memory_space=pl.ANY)
    dma = pltpu.SemaphoreType.DMA

    def scratch(*shape, dtype=BF16):
        return pltpu.VMEM(shape, dtype)

    result = pl.pallas_call(
        kernel,
        out_shape=jax.ShapeDtypeStruct((CROWS, D), F32),
        in_specs=[vmem] * 7 + [hbm] * 6,
        out_specs=vmem,
        scratch_shapes=[
            *[scratch(ROWS, HALF, dtype=F32)] * 4,
            scratch(CROWS, D, dtype=F32),
            *[scratch(4, ROWS, HD, dtype=F32)] * 2,
            scratch(HALF, 512), scratch(256, HALF), scratch(FFB, HALF), scratch(HALF, FFB), scratch(HALF, FFB),
            scratch(4, 16, ROWS, HALF), scratch(16, ROWS, HALF),
            scratch(3, 2, 4, ROWS, QUART), scratch(3, 2, 4, ROWS, HALF),
            scratch(3, 2, ROWS, QUART), scratch(3, 2, ROWS, HALF),
            scratch(2, GROUP, 512, dtype=F32), scratch(2, GROUP, 512), scratch(2, GROUP, 512),
            scratch(2, GROUP, 256), scratch(2, GROUP, HD), scratch(2, GROUP, HD),
            scratch(2, 2, GROUP, GROUP, dtype=F32), scratch(16, ROWS, 256),
            scratch(2, GROUP, 256, dtype=F32), scratch(2, GROUP, 256), scratch(2, GROUP, 256),
            scratch(16, ROWS, 512),
            scratch(3, 2, GROUP, FFB, dtype=F32), scratch(3, 2, GROUP, FFB), scratch(3, 2, GROUP, FFB),
            scratch(2, 16, ROWS, FFB),
            *[dma((2,))] * 2, *[dma((4,))] * 2, *[dma((7,))] * 2, *[dma((20,))] * 2,
            *[dma((4, 20))] * 2, *[dma((3, 20))] * 2, *[dma((10,))] * 2,
        ],
        compiler_params=pltpu.CompilerParams(
            collective_id=0, has_side_effects=True, vmem_limit_bytes=63 << 20
        ),
        cost_estimate=pl.CostEstimate(flops=19_000_000_000, bytes_accessed=8_000_000, transcendentals=1_000_000),
    )(
        jnp.pad(embedded.astype(F32), pad),
        jnp.pad(upstream.astype(F32), pad),
        gain_attn[None, :],
        gain_ffn[None, :],
        *tables(),
        w_query, w_keyval, w_out, w_gate, w_up, w_down,
    )
    return (result[:LIVE] * suffix_mask[:, None].astype(F32)).astype(BF16)


def solution(mesh):
    placed = (
        P(("dp", "tp"), None),
        P(("dp", "tp"), None),
        P(("dp", "tp")),
        P(),
        P(),
        P("dp", "tp"),
        P("dp", "tp"),
        P("tp", "dp"),
        P("dp", "tp"),
        P("dp", "tp"),
        P("tp", "dp"),
    )
    return jax.shard_map(
        per_device, mesh=mesh, in_specs=placed, out_specs=P(("dp", "tp"), None), check_vma=False
    )
```

time: 806 us -> 260 us (0.32)
  waiting for transfers between devices: 541 us -> 0 us
  Pallas kernels: 0 us -> 255 us
  blocking collectives: 116 us -> 0 us
  matrix products: 57.9 us -> 0 us
  starting transfers between devices: 30.8 us -> 0 us
  local copies, waits for them, and re-layouts: 25.1 us -> 0.01 us
  between operations: 14.7 us -> 0.03 us
  other arithmetic: 14 us -> 3.72 us
    all_gather x10 -> x0, waiting for transfers between devices: 533 us -> none  [the longest x4 107 us: spread(): return lax.all_gather(rows, 'tp', axis=0, tiled=True)]
    pallas_call x0 -> x1, Pallas kernels: none -> 255 us  [per_device(): pl.pallas_call(kernel, out_shape=jax.ShapeDtypeStruct((CROWS, D), F32), i...]
    unnamed x3 -> x0, blocking collectives: 116 us -> none
    dot_general x15 -> x0, matrix products: 56.7 us -> none  [the longest x6 34.6 us: times_transposed(): lax.dot_general(left, right, (((1,), (1,)), ((), ())), preferred_element_...]
    unnamed x9 -> x0, starting transfers between devices: 27.8 us -> none
    unnamed x51 -> x2, local copies, waits for them, and re-layouts: 23.3 us -> 0.01 us
    unnamed x19 -> x0, waiting for transfers between devices: 8.43 us -> none
  transfers between devices with their start and end apart: 21 -> 0, of which waited for: 12 -> 0; matrix products, arithmetic and copies ran while one was open for 11% -> 0% of each run, Pallas kernels for 0% -> 0%
where the time goes in v1:
time: 260 us; the launch traced here: 259 us
  Pallas kernels  255 us (98%)
  other arithmetic  3.72 us (1%)
    pallas_call x1, Pallas kernels, per_device(): pl.pallas_call(kernel, out_shape=jax.ShapeDtypeStruct((CROWS, D), F32), i...  255 us

profile of v1, /device:TPU:1, one launch (start us, length us, event | category | flops | bytes accessed | tf_op | source)
XLA Modules:
  0.0 259.2 jit_solution(8646841994548627132)
XLA Ops:
  0.0 2.0 pad_convert_fusion
  2.0 0.0 copy-start
  2.0 255.5 %shard_map.136 = f32[24,4096]{1,0:T(8,128)} custom-call(f32[24,4096]{1,0:T(8,128)} %get-tuple-element.6.emb, f32[24,4096]{1,0:T(8,128)} %get-tuple-element.5.ups, f32[1,4096]{1,0:T(1,128)} %bitcast.2, f32[1,4096]{1,0:T(1,128)} %bitcast.3, f32[192,128]{1,0:T(8,128)} %constant.10.clone.cos_ref, f32[192,128]{1,0:T(8,128)} %constant.11.clone.sin_ref, ...), custom_call_target="tpu_custom_call" | custom-call | flops 19000000512 | bytes 8000000 | tf_op jit(solution)/shard_map/pallas_call | solution.py:579
  257.4 0.0 copy-done
  257.4 1.8 multiply_convert_fusion
  (1 shorter events, 0.0 us)
Async XLA Ops:
  2.0 255.5 %copy-start = (s32[20]{0:T(128)S(1)}, s32[20]{0:T(128)}, u32[]{:S(2)}) copy-start(s32[20]{0:T(128)} %param.16) | copy-start | bytes 244

commit v2 on v1

v2 whole, which is shorter than its diff:
```python
import functools

import jax
import jax.numpy as jnp
import numpy as np
from jax import lax
from jax.experimental import pallas as pl
from jax.experimental.pallas import tpu as pltpu
from jax.sharding import PartitionSpec as P

MESH = pl.DeviceIdType.MESH
D = 4096
HALF = 2048
QUART = 1024
FFB = 896
HD = 128
SEQ = 40
ROWS = 48
CROWS = 24
LIVE = 20
GROUP = 4 * ROWS
CUTS = 4
F32 = jnp.float32
BF16 = jnp.bfloat16


def schedule():
    table = {}

    def put(point, what, who, *pieces):
        for i in pieces:
            i, n = i if isinstance(i, tuple) else (i, 0)
            table.setdefault(point, []).append((what, who, i, n))

    put("start", "y1", "diag", 0, 1)
    put("ups", "swap", "off", (2, 0), (2, 1), (2, 2), (2, 3), (3, 0), (3, 1), (3, 2), (3, 3), (4, 0), (4, 1), (4, 2), (4, 3))
    put("ag0.t0", "y1", "off", 0, 1)
    put("ag0.t1", "y2", "all", 0, 1)
    put("ag0.t1", "y1", "diag", 2, 3)
    put("ag0.f0", "y1", "diag", 4)
    put("ag0", "y1", "off", 2)
    put("ag1.t0", "y1", "off", 3)
    put("ag1.t2", "y2", "diag", 2)
    put("ag1.f3", "y1", "off", 4)
    put("ag1.f3", "y2", "off", 2)
    put("rs0.t1", "y2", "diag", 3)
    put("rs0", "y2", "diag", 4)
    put("rs0", "y2", "off", 3)
    put("mid", "y2", "off", 4)
    return table


SCHEDULE = schedule()


def dot_nn(left, right):
    return jnp.dot(left, right, preferred_element_type=F32)


def dot_nt(left, right):
    return lax.dot_general(left, right, (((1,), (1,)), ((), ())), preferred_element_type=F32)


def dot_tn(left, right):
    return lax.dot_general(left, right, (((0,), (0,)), ((), ())), preferred_element_type=F32)


def device_of(x, y, z, core):
    return ((x // 2) * 4 + y, (x % 2) * 8 + z * 2 + core)


def remote(src, dst, send_sem, recv_sem, device):
    return pltpu.make_async_remote_copy(
        src_ref=src, dst_ref=dst, send_sem=send_sem, recv_sem=recv_sem, device_id=device, device_id_type=MESH
    )


def arrived(dst, sem):
    pltpu.make_async_copy(dst, dst, sem).wait()


def kernel(
    emb_in, ups_in, gain_a, gain_f, cos_ref, sin_ref, mask_ref,
    w_q, w_kv, w_o, w_g, w_u, w_d,
    out_ref,
    emb, ups,
    xbuf, ubuf, mbuf, gbuf, fin, st_src, st_dst,
    wqkv, wo, wd, wg, wu,
    acts, part, rs_a, rs_b, rs_c, rs_d,
    qkv_own, qkv_send, qkv_recv, qb, kb, vb, probs, ctx, dctx_own, dctx_send, dctx_recv, dqkv,
    ffn_own, ffn_send, ffn_recv, ggu,
    ex_s, ex_r, st_s, st_r, x_s, x_r, y_s, y_r, ag_s, ag_r, rs_s, rs_r, cx_s, cx_r,
):
    dp, tp = lax.axis_index("dp"), lax.axis_index("tp")
    x_hi, y = dp // 4, dp % 4
    x_lo, z, core = tp // 8, (tp // 2) % 4, tp % 2
    x = x_hi * 2 + x_lo
    other = 1 - core
    partner = device_of(x, y, z, other)
    across_same = device_of((x + 2) % 4, y, z, core)
    across_other = device_of((x + 2) % 4, y, z, other)
    y_up = device_of(x, (y + 1) % 4, z, core)
    y_dn = device_of(x, (y + 3) % 4, z, core)

    def ring(is_x, step):
        return device_of((x + step * is_x) % 4, y, (z + step * (1 - is_x)) % 4, core)

    x_up, x_dn, z_up, z_dn = ring(1, 1), ring(1, 3), ring(0, 1), ring(0, 3)

    class Axes:
        def __init__(self, turn):
            self.r1_up, self.r1_dn = ring(turn, 1), ring(turn, 3)
            self.r2_up, self.r2_dn = ring(1 - turn, 1), ring(1 - turn, 3)
            self.p1 = turn * x + (1 - turn) * z
            self.p2 = turn * z + (1 - turn) * x
            self.turn = turn

        def slot(self, a, b):
            return ((self.p1 + a) % 4) * (1 + 3 * self.turn) + ((self.p2 + b) % 4) * (4 - 3 * self.turn)

    mixed = Axes(core)
    me = x * 4 + z
    diag = core == x_hi
    col0 = pl.multiple_of(core * HALF, HALF)
    col1 = pl.multiple_of(other * HALF, HALF)
    row0 = pl.multiple_of(core * CROWS, CROWS)

    barrier = pltpu.get_barrier_semaphore()
    friends = (partner, across_same, across_other, y_up, y_dn, x_up, x_dn, z_up, z_dn)
    for friend in friends:
        pl.semaphore_signal(barrier, inc=1, device_id=friend, device_id_type=MESH)
    for wide, given in ((emb, emb_in), (ups, ups_in)):
        wide[pl.ds(LIVE // 8 * 8, 8)] = jnp.zeros((8, D), F32)
        wide[pl.ds(0, LIVE)] = given[...].astype(F32)
    pl.semaphore_wait(barrier, len(friends))

    ex = []
    for i, (src, dst) in enumerate(((emb, xbuf), (ups, ubuf))):
        copy = remote(src.at[:, pl.ds(col1, HALF)], dst.at[pl.ds(row0, CROWS)], ex_s.at[i], ex_r.at[i], partner)
        copy.start()
        ex.append(copy)

    yrow = pl.multiple_of(y * 512, 512)
    kvcol = pl.multiple_of(256 + core * HD, HD)
    own_parts = (
        (w_q, wqkv.at[pl.ds(yrow, 512), pl.ds(0, 256)]),
        (w_o, wo.at[:, pl.ds(yrow, 512)]),
        (w_d, wd.at[:, pl.ds(yrow, 512)]),
        (w_g, wg.at[pl.ds(yrow, 512)]),
        (w_u, wu.at[pl.ds(yrow, 512)]),
    )
    kv_part = wqkv.at[pl.ds(yrow, 512), pl.ds(kvcol, HD)]
    k_part = wqkv.at[pl.ds(yrow, 512), pl.ds(256, HD)]
    v_part = wqkv.at[pl.ds(yrow, 512), pl.ds(256 + HD, HD)]

    def swap_cut(i, n):
        src, dst = own_parts[i]
        if i < 2:
            return src, dst, i
        rows = (FFB if i == 2 else 512) // CUTS
        return src.at[pl.ds(n * rows, rows)], dst.at[pl.ds(n * rows, rows)], 4 + CUTS * (i - 2) + n

    def cuts(i):
        return range(1 if i < 2 else CUTS)

    def swap_local(i):
        @pl.when(diag)
        def _():
            for n in cuts(i):
                src, dst, sem = swap_cut(i, n)
                pltpu.make_async_copy(src, dst, x_r.at[sem]).start()

    def swap_remote(i, n=0):
        src, dst, sem = swap_cut(i, n)

        @pl.when(jnp.logical_not(diag))
        def _():
            remote(src, dst, x_s.at[sem], x_r.at[sem], across_other).start()

    def swap_wait(i):
        for n in cuts(i):
            _, dst, sem = swap_cut(i, n)
            arrived(dst, x_r.at[sem])

    def swap_drain(i):
        @pl.when(jnp.logical_not(diag))
        def _():
            for n in cuts(i):
                src, dst, sem = swap_cut(i, n)
                remote(src, dst, x_s.at[sem], x_r.at[sem], across_other).wait_send()

    def kv_start():
        @pl.when(diag)
        def _():
            pltpu.make_async_copy(w_kv, kv_part, x_r.at[2 + core]).start()
            remote(w_kv, kv_part, x_s.at[3], x_r.at[2 + core], across_same).start()

        @pl.when(jnp.logical_not(diag))
        def _():
            remote(w_kv, kv_part, x_s.at[2], x_r.at[2 + core], partner).start()
            remote(w_kv, kv_part, x_s.at[3], x_r.at[2 + core], across_other).start()

    def kv_wait():
        arrived(k_part, x_r.at[2])
        arrived(v_part, x_r.at[3])

    def kv_drain():
        @pl.when(jnp.logical_not(diag))
        def _():
            remote(w_kv, kv_part, x_s.at[2], x_r.at[2 + core], partner).wait_send()

        remote(w_kv, kv_part, x_s.at[3], x_r.at[2 + core], across_same).wait_send()

    def piece(i, at, half=None):
        base = pl.multiple_of((at % 4) * 512, 512)
        if i in (1, 2):
            buf, rows = (wo, 256) if i == 1 else (wd, FFB)
            if half is None:
                return buf.at[:, pl.ds(base, 512)]
            return buf.at[pl.ds(half * rows // 2, rows // 2), pl.ds(base, 512)]
        buf = {0: wqkv, 3: wg, 4: wu}[i]
        if half is None:
            return buf.at[pl.ds(base, 512)]
        return buf.at[pl.ds(base + half * 256, 256)]

    def y1_copies(i):
        ref = piece(i, y)
        return (
            remote(ref, ref, y_s.at[4 * i], y_r.at[4 * i], y_up),
            remote(ref, ref, y_s.at[4 * i + 1], y_r.at[4 * i + 1], y_dn),
        )

    def y2_copies(i):
        from_dn, from_up = piece(i, y + 3, 0), piece(i, y + 1, 1)
        return (
            remote(from_dn, from_dn, y_s.at[4 * i + 2], y_r.at[4 * i + 2], y_up),
            remote(from_up, from_up, y_s.at[4 * i + 3], y_r.at[4 * i + 3], y_dn),
        )

    def y1_start(i):
        for copy in y1_copies(i):
            copy.start()

    def y2_start(i):
        up, dn = y2_copies(i)
        arrived(piece(i, y + 3), y_r.at[4 * i])
        up.start()
        arrived(piece(i, y + 1), y_r.at[4 * i + 1])
        dn.start()

    def y_finish(i):
        arrived(piece(i, y + 2, 0), y_r.at[4 * i + 2])
        arrived(piece(i, y + 2, 1), y_r.at[4 * i + 3])

    def y_drain(i):
        for copy in (*y1_copies(i), *y2_copies(i)):
            copy.wait_send()

    def pump(point):
        for what, who, i, n in SCHEDULE.get(point, ()):
            def act():
                if what == "swap":
                    swap_remote(i, n)
                elif what == "y1":
                    if i == 0:
                        kv_wait()
                    swap_wait(i)
                    y1_start(i)
                else:
                    y2_start(i)

            if who == "diag":
                pl.when(diag)(act)
            elif who == "off":
                pl.when(jnp.logical_not(diag))(act)
            else:
                act()

    def ag_copy(k, ref, n_send, n_recv, device):
        return remote(ref, ref, ag_s.at[k, n_send], ag_r.at[k, n_recv], device)

    def ag_refs(k, index):
        full = acts.at[k, index]
        return full, acts.at[k, index, :, pl.ds(0, QUART)], acts.at[k, index, :, pl.ds(QUART, QUART)]

    offs = (0, 3, 1, 2)

    def ag_get(k, axes, name, j=0):
        mine = ag_refs(k, axes.slot(offs[j], 0))[0]
        at = 4 + 4 * j
        if name == "a":
            return ag_copy(k, ag_refs(k, me)[0], 0, 0, axes.r1_up)
        if name == "b":
            return ag_copy(k, ag_refs(k, me)[0], 1, 1, axes.r1_dn)
        if name == "c":
            return ag_copy(k, ag_refs(k, axes.slot(3, 0))[1], 2, 2, axes.r1_up)
        if name == "d":
            return ag_copy(k, ag_refs(k, axes.slot(1, 0))[2], 3, 3, axes.r1_dn)
        if name == "up":
            return ag_copy(k, mine, at, at, axes.r2_up)
        if name == "dn":
            return ag_copy(k, mine, at + 1, at + 1, axes.r2_dn)
        if name == "up2":
            return ag_copy(k, ag_refs(k, axes.slot(offs[j], 3))[1], at + 2, at + 2, axes.r2_up)
        return ag_copy(k, ag_refs(k, axes.slot(offs[j], 1))[2], at + 3, at + 3, axes.r2_dn)

    def ag_first(k, axes):
        ag_get(k, axes, "a").start()
        ag_get(k, axes, "b").start()

    def ag_across(k, axes, j):
        ag_get(k, axes, "up", j).start()
        ag_get(k, axes, "dn", j).start()

    def ag_start(k, axes):
        ag_first(k, axes)
        ag_across(k, axes, 0)

    def ag_next(k, axes, across=True):
        arrived(ag_refs(k, axes.slot(3, 0))[0], ag_r.at[k, 0])
        ag_get(k, axes, "c").start()
        if across:
            ag_across(k, axes, 1)
        pump(f"ag{k}.0")
        arrived(ag_refs(k, axes.slot(1, 0))[0], ag_r.at[k, 1])
        ag_get(k, axes, "d").start()
        if across:
            ag_across(k, axes, 2)
        pump(f"ag{k}.1")

    def ag_rest(k, axes):
        def through(j):
            arrived(ag_refs(k, axes.slot(offs[j], 3))[0], ag_r.at[k, 4 + 4 * j])
            ag_get(k, axes, "up2", j).start()
            arrived(ag_refs(k, axes.slot(offs[j], 1))[0], ag_r.at[k, 5 + 4 * j])
            ag_get(k, axes, "dn2", j).start()
            pump(f"ag{k}.t{j}")

        through(0)
        arrived(ag_refs(k, axes.slot(2, 0))[1], ag_r.at[k, 2])
        arrived(ag_refs(k, axes.slot(2, 0))[2], ag_r.at[k, 3])
        ag_across(k, axes, 3)
        pump(f"ag{k}.2")
        for j in (1, 2, 3):
            through(j)
        for j in range(4):
            far = ag_refs(k, axes.slot(offs[j], 2))
            arrived(far[1], ag_r.at[k, 6 + 4 * j])
            arrived(far[2], ag_r.at[k, 7 + 4 * j])
            pump(f"ag{k}.f{j}")
        for name in ("a", "b", "c", "d"):
            ag_get(k, axes, name).wait_send()
        for j in range(4):
            for name in ("up", "dn", "up2", "dn2"):
                ag_get(k, axes, name, j).wait_send()

    def rs_run(k, compute):
        def send(src, dst, n, device):
            copy = remote(src, dst, rs_s.at[k, n], rs_r.at[k, n], device)
            copy.start()
            return copy

        lo, hi = pl.ds(0, QUART), pl.ds(QUART, QUART)
        sent = []
        compute(2)
        for i in (2, 1, 3, 0):
            at = mixed.slot(i, 2)
            sent.append(send(part.at[at, :, lo], rs_a.at[k, 0, i], 2 * i, mixed.r2_up))
            sent.append(send(part.at[at, :, hi], rs_a.at[k, 1, i], 2 * i + 1, mixed.r2_dn))
        pump(f"rs{k}.0")
        compute(1)
        compute(3)
        for i in (2, 1, 3, 0):
            at = mixed.slot(i, 1)
            arrived(rs_a.at[k, 0, i], rs_r.at[k, 2 * i])
            part[at, :, lo] = (part[at, :, lo].astype(F32) + rs_a[k, 0, i].astype(F32)).astype(BF16)
            sent.append(send(part.at[at], rs_b.at[k, 0, i], 8 + 2 * i, mixed.r2_up))
            at = mixed.slot(i, 3)
            arrived(rs_a.at[k, 1, i], rs_r.at[k, 2 * i + 1])
            part[at, :, hi] = (part[at, :, hi].astype(F32) + rs_a[k, 1, i].astype(F32)).astype(BF16)
            sent.append(send(part.at[at], rs_b.at[k, 1, i], 9 + 2 * i, mixed.r2_dn))
            pump(f"rs{k}.t{i}")
        compute(0)
        pump(f"rs{k}.1")

        def add_both(i):
            at = mixed.slot(i, 0)
            arrived(rs_b.at[k, 0, i], rs_r.at[k, 8 + 2 * i])
            arrived(rs_b.at[k, 1, i], rs_r.at[k, 9 + 2 * i])
            return part[at].astype(F32) + rs_b[k, 0, i].astype(F32) + rs_b[k, 1, i].astype(F32)

        at = mixed.slot(2, 0)
        part[at] = add_both(2).astype(BF16)
        sent.append(send(part.at[at, :, lo], rs_c.at[k, 0], 16, mixed.r1_up))
        sent.append(send(part.at[at, :, hi], rs_c.at[k, 1], 17, mixed.r1_dn))
        at = mixed.slot(1, 0)
        part[at] = add_both(1).astype(BF16)
        arrived(rs_c.at[k, 0], rs_r.at[k, 16])
        part[at, :, lo] = (part[at, :, lo].astype(F32) + rs_c[k, 0].astype(F32)).astype(BF16)
        sent.append(send(part.at[at], rs_d.at[k, 0], 18, mixed.r1_up))
        at = mixed.slot(3, 0)
        part[at] = add_both(3).astype(BF16)
        arrived(rs_c.at[k, 1], rs_r.at[k, 17])
        part[at, :, hi] = (part[at, :, hi].astype(F32) + rs_c[k, 1].astype(F32)).astype(BF16)
        sent.append(send(part.at[at], rs_d.at[k, 1], 19, mixed.r1_dn))
        pump(f"rs{k}.2")
        total = add_both(0)
        arrived(rs_d.at[k, 0], rs_r.at[k, 18])
        arrived(rs_d.at[k, 1], rs_r.at[k, 19])
        total = total + rs_d[k, 0].astype(F32) + rs_d[k, 1].astype(F32)
        for copy in sent:
            copy.wait_send()
        return total

    def both_halves(i, value):
        mine = jnp.broadcast_to(jnp.sum(value, axis=-1, keepdims=True), (ROWS, HD))
        st_src[i] = mine
        copy = remote(st_src.at[i], st_dst.at[i], st_s.at[i], st_r.at[i], partner)
        copy.start()
        copy.wait()
        return (mine + st_dst[i])[:, :1] * (1.0 / D)

    def group_rows(ref, at):
        return jnp.concatenate([ref[mixed.slot(i, at)] for i in range(4)], axis=0)

    def swap_rows(op, i, src, dst):
        return remote(src, dst, cx_s.at[2 * op + i], cx_r.at[2 * op + i], partner)

    def halves_matmul(op, k, weights_fn, send_ref, recv_ref, own_ref):
        def theirs(i, carry):
            rows = acts[k, pl.ds(8 * other + 4 * i, 4)].reshape(GROUP, HALF)
            send_ref[i] = weights_fn(rows).astype(BF16)
            swap_rows(op, i, send_ref.at[i], recv_ref.at[i]).start()
            return carry

        def ours(i, carry):
            rows = acts[k, pl.ds(8 * core + 4 * i, 4)].reshape(GROUP, HALF)
            own_ref[i] = weights_fn(rows)
            return carry

        lax.fori_loop(0, 2, theirs, 0)
        lax.fori_loop(0, 2, ours, 0)

    def swap_done(op, send_ref):
        for i in range(2):
            swap_rows(op, i, send_ref.at[i], send_ref.at[i]).wait_send()

    def quad(who, i):
        return pl.ds(8 * who + 4 * i, 4)

    def rows_start(op, i, ref):
        swap_rows(op, i, ref.at[quad(core, i)], ref.at[quad(core, i)]).start()

    def rows_wait(op, ref):
        for i in range(2):
            arrived(ref.at[quad(other, i)], cx_r.at[2 * op + i])
        for i in range(2):
            swap_rows(op, i, ref.at[quad(core, i)], ref.at[quad(core, i)]).wait_send()

    def rope(value, sign):
        return value * cos_ref[...] + sign * pltpu.roll(value, HD // 2, 1) * sin_ref[...]

    swap_remote(0)
    kv_start()
    swap_remote(1)
    for i in range(5):
        swap_local(i)
    pump("start")
    gain_attn = gain_a[:, pl.ds(col0, HALF)]
    gain_ffn = gain_f[:, pl.ds(col0, HALF)]
    xbuf[pl.ds(row0, CROWS)] = emb[:, pl.ds(col0, HALF)]
    ubuf[pl.ds(row0, CROWS)] = ups[:, pl.ds(col0, HALF)]
    ex[0].wait()
    inputs = xbuf[...]
    r_attn = lax.rsqrt(both_halves(0, inputs * inputs) + 1e-05)
    acts[0, me] = (inputs * r_attn * gain_attn).astype(BF16)
    along = Axes(1)
    ag_start(0, along)
    ex[1].wait()
    acts[1, me] = ubuf[...].astype(BF16)
    ag_first(1, along)
    pump("norm")
    ag_next(0, along)
    ag_next(1, along, across=False)
    pump("ups")
    ag_rest(0, along)
    pump("ag0")
    for j in range(3):
        ag_across(1, along, j)
    pump("ag1")
    y_finish(0)

    halves_matmul(0, 0, lambda rows: dot_nn(rows, wqkv[...]), qkv_send, qkv_recv, qkv_own)
    scale = 1.0 / HD**0.5

    def attend(g, carry):
        arrived(qkv_recv.at[g], cx_r.at[g])
        total = qkv_own[g] + qkv_recv[g].astype(F32)
        keys = rope(total[:, 256:384], 1.0).astype(BF16)
        values = total[:, 384:].astype(BF16)
        kb[g] = keys
        vb[g] = values
        for h in range(2):
            cols = slice(h * HD, (h + 1) * HD)
            query = rope(total[:, cols], 1.0).astype(BF16)
            qb[g, :, cols] = query
            scores = jnp.where(mask_ref[...] > 0, dot_nt(query, keys) * scale, -1e30)
            expo = jnp.exp(scores - jnp.max(scores, axis=-1, keepdims=True))
            prob = expo / jnp.sum(expo, axis=-1, keepdims=True)
            probs[g, h] = prob
            out = dot_nn(prob.astype(BF16), values).astype(BF16)
            ctx[quad(core, g), :, cols] = out.reshape(4, ROWS, HD)
        rows_start(5, g, ctx)
        return carry

    lax.fori_loop(0, 2, attend, 0)
    swap_done(0, qkv_send)
    ag_rest(1, along)
    y_finish(1)
    rows_wait(5, ctx)

    def spread_group(at, term):
        def step(n, carry):
            cols = pl.ds(pl.multiple_of(n * 512, 512), 512)
            value = term(cols).astype(BF16)
            for i in range(4):
                part[mixed.slot(i, at), :, cols] = value[i * ROWS:(i + 1) * ROWS]
            return carry

        lax.fori_loop(0, 4, step, 0)

    def out_term(at):
        rows = group_rows(ctx, at)
        spread_group(at, lambda cols: dot_nn(rows, wo[:, cols]))

    middle = inputs + rs_run(0, out_term)
    mbuf[...] = middle
    pump("rs0")
    r_ffn = lax.rsqrt(both_halves(1, middle * middle) + 1e-05)
    acts[2, me] = (middle * r_ffn * gain_ffn).astype(BF16)
    ag_start(2, mixed)
    pump("mid")
    ag_next(2, mixed)
    ag_rest(2, mixed)
    pump("ag2")

    def ffn_part(j, k, weights_fn):
        halves_matmul(1 + j, k, weights_fn, ffn_send.at[j], ffn_recv.at[j], ffn_own.at[j])

    y_finish(2)
    ffn_part(0, 1, lambda rows: dot_nt(rows, wd[...]))
    pump("hidden")
    y_finish(3)
    ffn_part(1, 2, lambda rows: dot_nn(rows, wg[...]))
    pump("gate")
    y_finish(4)
    ffn_part(2, 2, lambda rows: dot_nn(rows, wu[...]))

    def gates(g, carry):
        for j in range(3):
            arrived(ffn_recv.at[j, g], cx_r.at[2 + 2 * j + g])

        def gate_rows(i, inner):
            rows = pl.ds(pl.multiple_of(i * ROWS, ROWS), ROWS)
            hidden, gate, up = (ffn_own[j, g, rows] + ffn_recv[j, g, rows].astype(F32) for j in range(3))
            sigm = jax.nn.sigmoid(gate)
            lifted = hidden * sigm
            at = 8 * core + 4 * g + i
            ggu[0, at] = (lifted * up * (1.0 + gate * (1.0 - sigm))).astype(BF16)
            ggu[1, at] = (lifted * gate).astype(BF16)
            return inner

        lax.fori_loop(0, 4, gate_rows, 0)
        for j in range(2):
            rows_start(6 + j, g, ggu.at[j])
        return carry

    lax.fori_loop(0, 2, gates, 0)
    for j in range(3):
        swap_done(1 + j, ffn_send.at[j])
    for j in range(2):
        rows_wait(6 + j, ggu.at[j])

    def ffn_term(at):
        gate_rows, up_rows = group_rows(ggu.at[0], at), group_rows(ggu.at[1], at)
        spread_group(at, lambda cols: dot_nt(gate_rows, wg[cols]) + dot_nt(up_rows, wu[cols]))

    scaled = rs_run(1, ffn_term) * gain_ffn
    middle = mbuf[...]
    mean = both_halves(2, scaled * middle)
    grad_mid = ubuf[...] + r_ffn * scaled - middle * r_ffn**3 * mean
    gbuf[...] = grad_mid
    acts[3, me] = grad_mid.astype(BF16)
    ag_start(3, mixed)
    ag_next(3, mixed)
    ag_rest(3, mixed)

    halves_matmul(4, 3, lambda rows: dot_nt(rows, wo[...]), dctx_send, dctx_recv, dctx_own)

    def attend_back(g, carry):
        arrived(dctx_recv.at[g], cx_r.at[8 + g])
        upper = (dctx_own[g] + dctx_recv[g].astype(F32)).astype(BF16)
        keys, values = kb[g], vb[g]
        here = quad(core, g)
        grad_keys = jnp.zeros((GROUP, HD), F32)
        grad_values = jnp.zeros((GROUP, HD), F32)
        for h in range(2):
            cols = slice(h * HD, (h + 1) * HD)
            prob = probs[g, h]
            grad_probs = dot_nt(upper[:, cols], values)
            grad_scores = (
                prob * (grad_probs - jnp.sum(grad_probs * prob, axis=-1, keepdims=True)) * scale
            ).astype(BF16)
            grad_query = rope(dot_nn(grad_scores, keys), -1.0).astype(BF16)
            dqkv[here, :, cols] = grad_query.reshape(4, ROWS, HD)
            grad_keys += dot_tn(grad_scores, qb[g, :, cols])
            grad_values += dot_tn(prob.astype(BF16), upper[:, cols])
        dqkv[here, :, 256:384] = rope(grad_keys, -1.0).astype(BF16).reshape(4, ROWS, HD)
        dqkv[here, :, 384:] = grad_values.astype(BF16).reshape(4, ROWS, HD)
        rows_start(8, g, dqkv)
        return carry

    lax.fori_loop(0, 2, attend_back, 0)
    swap_done(4, dctx_send)
    rows_wait(8, dqkv)

    def attn_term(at):
        rows = group_rows(dqkv, at)
        spread_group(at, lambda cols: dot_nt(rows, wqkv[cols]))

    scaled = rs_run(2, attn_term) * gain_attn
    inputs = xbuf[...]
    mean = both_halves(3, scaled * inputs)
    mbuf[...] = gbuf[...] + r_attn * scaled - inputs * r_attn**3 * mean
    row1 = pl.multiple_of(other * CROWS, CROWS)
    copy = swap_rows(9, 0, mbuf.at[pl.ds(row1, CROWS)], fin.at[:, pl.ds(col0, HALF)])
    copy.start()
    fin[:, pl.ds(col0, HALF)] = mbuf[pl.ds(row0, CROWS)]
    for i in range(5):
        swap_drain(i)
        y_drain(i)
    kv_drain()
    copy.wait()
    out_ref[...] = fin[...]


def tables():
    place = np.arange(ROWS) % CROWS
    spot = np.minimum(place, LIVE - 1) + LIVE * (np.arange(ROWS) // CROWS)
    freqs = np.float32(500000.0) ** (-np.arange(HD // 2, dtype=np.float32) * np.float32(2.0 / HD))
    angles = spot.astype(np.float32)[:, None] * freqs[None, :]
    cosine, sine = np.cos(angles), np.sin(angles)
    cosine = np.tile(np.concatenate([cosine, cosine], axis=1), (4, 1)).astype(np.float32)
    sine = np.tile(np.concatenate([-sine, sine], axis=1), (4, 1)).astype(np.float32)
    cand = np.arange(GROUP) // ROWS
    spots, live = np.tile(spot, 4), np.tile(place < LIVE, 4)
    mask = (cand[:, None] == cand[None, :]) & live[None, :] & (spots[:, None] >= spots[None, :])
    return cosine, sine, mask.astype(np.float32)


def per_device(embedded, upstream, suffix_mask, gain_attn, gain_ffn, w_query, w_keyval, w_out, w_gate, w_up, w_down):
    vmem = pl.BlockSpec(memory_space=pltpu.VMEM)
    hbm = pl.BlockSpec(memory_space=pl.ANY)
    dma = pltpu.SemaphoreType.DMA

    def scratch(*shape, dtype=BF16):
        return pltpu.VMEM(shape, dtype)

    result = pl.pallas_call(
        kernel,
        out_shape=jax.ShapeDtypeStruct((CROWS, D), F32),
        in_specs=[vmem] * 7 + [hbm] * 6,
        out_specs=vmem,
        scratch_shapes=[
            *[scratch(CROWS, D, dtype=F32)] * 2,
            *[scratch(ROWS, HALF, dtype=F32)] * 4,
            scratch(CROWS, D, dtype=F32),
            *[scratch(4, ROWS, HD, dtype=F32)] * 2,
            scratch(HALF, 512), scratch(256, HALF), scratch(FFB, HALF), scratch(HALF, FFB), scratch(HALF, FFB),
            scratch(4, 16, ROWS, HALF), scratch(16, ROWS, HALF),
            scratch(3, 2, 4, ROWS, QUART), scratch(3, 2, 4, ROWS, HALF),
            scratch(3, 2, ROWS, QUART), scratch(3, 2, ROWS, HALF),
            scratch(2, GROUP, 512, dtype=F32), scratch(2, GROUP, 512), scratch(2, GROUP, 512),
            scratch(2, GROUP, 256), scratch(2, GROUP, HD), scratch(2, GROUP, HD),
            scratch(2, 2, GROUP, GROUP, dtype=F32), scratch(16, ROWS, 256),
            scratch(2, GROUP, 256, dtype=F32), scratch(2, GROUP, 256), scratch(2, GROUP, 256),
            scratch(16, ROWS, 512),
            scratch(3, 2, GROUP, FFB, dtype=F32), scratch(3, 2, GROUP, FFB), scratch(3, 2, GROUP, FFB),
            scratch(2, 16, ROWS, FFB),
            *[dma((2,))] * 2, *[dma((4,))] * 2, *[dma((4 + 3 * CUTS,))] * 2, *[dma((20,))] * 2,
            *[dma((4, 20))] * 2, *[dma((3, 20))] * 2, *[dma((20,))] * 2,
        ],
        compiler_params=pltpu.CompilerParams(
            collective_id=0, has_side_effects=True, vmem_limit_bytes=63 << 20
        ),
        cost_estimate=pl.CostEstimate(flops=19_000_000_000, bytes_accessed=8_000_000, transcendentals=1_000_000),
    )(
        embedded,
        upstream,
        gain_attn[None, :],
        gain_ffn[None, :],
        *tables(),
        w_query, w_keyval, w_out, w_gate, w_up, w_down,
    )
    return (result[:LIVE] * suffix_mask[:, None].astype(F32)).astype(BF16)


def solution(mesh):
    placed = (
        P(("dp", "tp"), None),
        P(("dp", "tp"), None),
        P(("dp", "tp")),
        P(),
        P(),
        P("dp", "tp"),
        P("dp", "tp"),
        P("tp", "dp"),
        P("dp", "tp"),
        P("dp", "tp"),
        P("tp", "dp"),
    )
    return jax.shard_map(
        per_device, mesh=mesh, in_specs=placed, out_specs=P(("dp", "tp"), None), check_vma=False
    )
```

time: 260 us -> 231 us (0.89)
  Pallas kernels: 255 us -> 228 us
    pallas_call x1, Pallas kernels: 255 us -> 228 us  [per_device(): pl.pallas_call(kernel, out_shape=jax.ShapeDtypeStruct((CROWS, D), F32), i...]
where the time goes in v2:
time: 231 us
  Pallas kernels  228 us (99%)
    pallas_call x1, Pallas kernels, per_device(): pl.pallas_call(kernel, out_shape=jax.ShapeDtypeStruct((CROWS, D), F32), i...  228 us

profile of v2, /device:TPU:1, one launch (start us, length us, event | category | flops | bytes accessed | tf_op | source)
XLA Modules:
  0.0 230.8 jit_solution(7375719958808433970)
XLA Ops:
  0.0 0.0 copy-start
  0.0 0.7 copy-done
  0.7 228.4 %shard_map.136 = f32[24,4096]{1,0:T(8,128)} custom-call(bf16[20,4096]{1,0:T(8,128)(2,1)} %emb_in.1, bf16[20,4096]{1,0:T(8,128)(2,1)} %ups_in.1, f32[1,4096]{1,0:T(1,128)} %bitcast.2, f32[1,4096]{1,0:T(1,128)} %bitcast.3, f32[192,128]{1,0:T(8,128)} %constant.6.clone.cos_ref, f32[192,128]{1,0:T(8,128)} %constant.7.clone.sin_ref, ...), custom_call_target="tpu_custom_call" | custom-call | flops 19000000512 | bytes 8000000 | tf_op jit(solution)/shard_map/pallas_call | solution.py:669
  229.0 1.8 multiply_convert_fusion
  (1 shorter events, 0.0 us)
Async XLA Ops:
  0.0 0.7 copy-start

commit v3 on v2

--- a/solution.py
+++ b/solution.py
@@ -32,21 +32,27 @@
             i, n = i if isinstance(i, tuple) else (i, 0)
             table.setdefault(point, []).append((what, who, i, n))
 
-    put("start", "y1", "diag", 0, 1)
-    put("ups", "swap", "off", (2, 0), (2, 1), (2, 2), (2, 3), (3, 0), (3, 1), (3, 2), (3, 3), (4, 0), (4, 1), (4, 2), (4, 3))
+    put("start", "y1", "diag", 1, 0, 2)
+    for i in (2, 3, 4):
+        put("ups", "swap", "off", *((i, n) for n in range(CUTS)))
     put("ag0.t0", "y1", "off", 0, 1)
     put("ag0.t1", "y2", "all", 0, 1)
-    put("ag0.t1", "y1", "diag", 2, 3)
+    put("ag0.t1", "y1", "diag", 3)
     put("ag0.f0", "y1", "diag", 4)
     put("ag0", "y1", "off", 2)
-    put("ag1.t0", "y1", "off", 3)
-    put("ag1.t2", "y2", "diag", 2)
-    put("ag1.f3", "y1", "off", 4)
-    put("ag1.f3", "y2", "off", 2)
-    put("rs0.t1", "y2", "diag", 3)
+    put("attend", "ag", "all", 1, 1)
+    put("attend", "y1", "off", 3)
+    put("attend", "y2", "diag", 2)
+    put("rs0.0", "ag", "all", 1)
+    put("rs0.t2", "ag", "all", 1)
+    put("rs0.t3", "ag", "all", 1)
+    put("rs0.t3", "y1", "off", 4)
+    put("rs0.1", "y2", "diag", 3)
+    put("rs0.1", "y2", "off", 2)
+    put("rs0", "ag", "all", 1, 1, 1, 1)
     put("rs0", "y2", "diag", 4)
-    put("rs0", "y2", "off", 3)
-    put("mid", "y2", "off", 4)
+    put("mid", "y2", "off", 3)
+    put("ag2.f0", "y2", "off", 4)
     return table
 
 
@@ -88,7 +94,7 @@
     wqkv, wo, wd, wg, wu,
     acts, part, rs_a, rs_b, rs_c, rs_d,
     qkv_own, qkv_send, qkv_recv, qb, kb, vb, probs, ctx, dctx_own, dctx_send, dctx_recv, dqkv,
-    ffn_own, ffn_send, ffn_recv, ggu,
+    ffn_own, ffn_send, ffn_recv, up_acc, ggu,
     ex_s, ex_r, st_s, st_r, x_s, x_r, y_s, y_r, ag_s, ag_r, rs_s, rs_r, cx_s, cx_r,
 ):
     dp, tp = lax.axis_index("dp"), lax.axis_index("tp")
@@ -256,11 +262,15 @@
         for copy in (*y1_copies(i), *y2_copies(i)):
             copy.wait_send()
 
+    later = {}
+
     def pump(point):
         for what, who, i, n in SCHEDULE.get(point, ()):
             def act():
                 if what == "swap":
                     swap_remote(i, n)
+                elif what == "ag":
+                    next(later[i])
                 elif what == "y1":
                     if i == 0:
                         kv_wait()
@@ -328,7 +338,7 @@
             ag_across(k, axes, 2)
         pump(f"ag{k}.1")
 
-    def ag_rest(k, axes):
+    def ag_steps(k, axes):
         def through(j):
             arrived(ag_refs(k, axes.slot(offs[j], 3))[0], ag_r.at[k, 4 + 4 * j])
             ag_get(k, axes, "up2", j).start()
@@ -337,22 +347,30 @@
             pump(f"ag{k}.t{j}")
 
         through(0)
+        yield
         arrived(ag_refs(k, axes.slot(2, 0))[1], ag_r.at[k, 2])
         arrived(ag_refs(k, axes.slot(2, 0))[2], ag_r.at[k, 3])
         ag_across(k, axes, 3)
         pump(f"ag{k}.2")
+        yield
         for j in (1, 2, 3):
             through(j)
+            yield
         for j in range(4):
             far = ag_refs(k, axes.slot(offs[j], 2))
             arrived(far[1], ag_r.at[k, 6 + 4 * j])
             arrived(far[2], ag_r.at[k, 7 + 4 * j])
             pump(f"ag{k}.f{j}")
+            yield
         for name in ("a", "b", "c", "d"):
             ag_get(k, axes, name).wait_send()
         for j in range(4):
             for name in ("up", "dn", "up2", "dn2"):
                 ag_get(k, axes, name, j).wait_send()
+
+    def ag_rest(k, axes):
+        for _ in ag_steps(k, axes):
+            pass
 
     def rs_run(k, compute):
         def send(src, dst, n, device):
@@ -487,6 +505,7 @@
     pump("ag0")
     for j in range(3):
         ag_across(1, along, j)
+    later[1] = ag_steps(1, along)
     pump("ag1")
     y_finish(0)
 
@@ -515,7 +534,7 @@
 
     lax.fori_loop(0, 2, attend, 0)
     swap_done(0, qkv_send)
-    ag_rest(1, along)
+    pump("attend")
     y_finish(1)
     rows_wait(5, ctx)
 
@@ -547,14 +566,36 @@
     def ffn_part(j, k, weights_fn):
         halves_matmul(1 + j, k, weights_fn, ffn_send.at[j], ffn_recv.at[j], ffn_own.at[j])
 
+    for _ in later[1]:
+        pass
     y_finish(2)
     ffn_part(0, 1, lambda rows: dot_nt(rows, wd[...]))
     pump("hidden")
     y_finish(3)
     ffn_part(1, 2, lambda rows: dot_nn(rows, wg[...]))
     pump("gate")
+    def up_depth(who, i, step):
+        depth = pl.ds(pl.multiple_of(((y + step) % 4) * 512, 512), 512)
+        return dot_nn(acts[2, quad(who, i), :, depth].reshape(GROUP, 512), wu[depth])
+
+    def up_first(i, carry):
+        up_acc[i] = up_depth(other, i, 0) + up_depth(other, i, 1) + up_depth(other, i, 3)
+        ffn_own[2, i] = up_depth(core, i, 0) + up_depth(core, i, 1) + up_depth(core, i, 3)
+        return carry
+
+    def up_theirs(i, carry):
+        ffn_send[2, i] = (up_acc[i] + up_depth(other, i, 2)).astype(BF16)
+        swap_rows(3, i, ffn_send.at[2, i], ffn_recv.at[2, i]).start()
+        return carry
+
+    def up_ours(i, carry):
+        ffn_own[2, i] = ffn_own[2, i] + up_depth(core, i, 2)
+        return carry
+
+    lax.fori_loop(0, 2, up_first, 0)
     y_finish(4)
-    ffn_part(2, 2, lambda rows: dot_nn(rows, wu[...]))
+    lax.fori_loop(0, 2, up_theirs, 0)
+    lax.fori_loop(0, 2, up_ours, 0)
 
     def gates(g, carry):
         for j in range(3):
@@ -629,19 +670,25 @@
         spread_group(at, lambda cols: dot_nt(rows, wqkv[cols]))
 
     scaled = rs_run(2, attn_term) * gain_attn
-    inputs = xbuf[...]
-    mean = both_halves(3, scaled * inputs)
-    mbuf[...] = gbuf[...] + r_attn * scaled - inputs * r_attn**3 * mean
+    sums = jnp.broadcast_to(jnp.sum(scaled * xbuf[...], axis=-1, keepdims=True), (ROWS, HD))
+    st_src[3] = sums
+    copies = [remote(st_src.at[3], st_dst.at[3], st_s.at[3], st_r.at[3], partner)]
+    mbuf[...] = gbuf[...] + r_attn * scaled
     row1 = pl.multiple_of(other * CROWS, CROWS)
-    copy = swap_rows(9, 0, mbuf.at[pl.ds(row1, CROWS)], fin.at[:, pl.ds(col0, HALF)])
-    copy.start()
+    copies.append(swap_rows(9, 0, mbuf.at[pl.ds(row1, CROWS)], fin.at[:, pl.ds(col0, HALF)]))
+    for copy in copies:
+        copy.start()
     fin[:, pl.ds(col0, HALF)] = mbuf[pl.ds(row0, CROWS)]
+    gbuf[:, :HD] = jnp.broadcast_to(r_attn, (ROWS, HD))
     for i in range(5):
         swap_drain(i)
         y_drain(i)
     kv_drain()
-    copy.wait()
-    out_ref[...] = fin[...]
+    for copy in copies:
+        copy.wait()
+    here = pl.ds(row0, CROWS)
+    mean = (st_src[3, here] + st_dst[3, here])[:, :1] * (1.0 / D)
+    out_ref[...] = fin[...] - emb[...] * (gbuf[here, :HD][:, :1] ** 3 * mean)
 
 
 def tables():
@@ -686,6 +733,7 @@
             scratch(2, GROUP, 256, dtype=F32), scratch(2, GROUP, 256), scratch(2, GROUP, 256),
             scratch(16, ROWS, 512),
             scratch(3, 2, GROUP, FFB, dtype=F32), scratch(3, 2, GROUP, FFB), scratch(3, 2, GROUP, FFB),
+            scratch(2, GROUP, FFB, dtype=F32),
             scratch(2, 16, ROWS, FFB),
             *[dma((2,))] * 2, *[dma((4,))] * 2, *[dma((4 + 3 * CUTS,))] * 2, *[dma((20,))] * 2,
             *[dma((4, 20))] * 2, *[dma((3, 20))] * 2, *[dma((20,))] * 2,

time: 231 us -> 217 us (0.939)
  Pallas kernels: 228 us -> 214 us
    pallas_call x1, Pallas kernels: 228 us -> 214 us  [per_device(): pl.pallas_call(kernel, out_shape=jax.ShapeDtypeStruct((CROWS, D), F32), i...]
where the time goes in v3:
time: 217 us
  Pallas kernels  214 us (99%)
    pallas_call x1, Pallas kernels, per_device(): pl.pallas_call(kernel, out_shape=jax.ShapeDtypeStruct((CROWS, D), F32), i...  214 us

profile of v3, /device:TPU:1, one launch (start us, length us, event | category | flops | bytes accessed | tf_op | source)
XLA Modules:
  0.0 216.7 jit_solution(12432143496518868931)
XLA Ops:
  0.0 0.0 copy-start
  0.0 0.7 copy-done
  0.7 214.3 %shard_map.136 = f32[24,4096]{1,0:T(8,128)} custom-call(bf16[20,4096]{1,0:T(8,128)(2,1)} %emb_in.1, bf16[20,4096]{1,0:T(8,128)(2,1)} %ups_in.1, f32[1,4096]{1,0:T(1,128)} %bitcast.2, f32[1,4096]{1,0:T(1,128)} %bitcast.3, f32[192,128]{1,0:T(8,128)} %constant.6.clone.cos_ref, f32[192,128]{1,0:T(8,128)} %constant.7.clone.sin_ref, ...), custom_call_target="tpu_custom_call" | custom-call | flops 19000000512 | bytes 8000000 | tf_op jit(solution)/shard_map/pallas_call | solution.py:716
  214.9 1.8 multiply_convert_fusion
  (1 shorter events, 0.0 us)
Async XLA Ops:
  0.0 0.7 copy-start

commit v4 on v3

--- a/solution.py
+++ b/solution.py
@@ -20,6 +20,9 @@
 LIVE = 20
 GROUP = 4 * ROWS
 CUTS = 4
+PACK = 5120
+PHALF = 2560
+DENSE = (0, 1, 0, 0)
 F32 = jnp.float32
 BF16 = jnp.bfloat16
 
@@ -71,6 +74,32 @@
     return lax.dot_general(left, right, (((0,), (0,)), ((), ())), preferred_element_type=F32)
 
 
+def top_rows(columns):
+    return lax.broadcasted_iota(jnp.int32, (8, columns), 0) < 4
+
+
+def squeeze(rows):
+    last = jnp.where(top_rows(rows.shape[1]), rows[16:24], pltpu.roll(rows[40:48], 4, 0))
+    return rows[0:8], rows[8:16], rows[24:32], rows[32:40], last
+
+
+def pack(rows):
+    tiles = [jnp.concatenate([tile[:, :QUART], tile[:, QUART:]], axis=0) for tile in squeeze(rows)]
+    return jnp.concatenate(tiles, axis=1).astype(BF16)
+
+
+def unpack(block):
+    block = block.astype(F32)
+    tiles = []
+    for i in range(5):
+        cols = slice(i * QUART, (i + 1) * QUART)
+        tiles.append(jnp.concatenate([block[:8, cols], block[8:, cols]], axis=1))
+    top = top_rows(HALF)
+    third = jnp.where(top, tiles[4], 0.0)
+    sixth = jnp.where(top, pltpu.roll(tiles[4], 4, 0), 0.0)
+    return jnp.concatenate([tiles[0], tiles[1], third, tiles[2], tiles[3], sixth], axis=0)
+
+
 def device_of(x, y, z, core):
     return ((x // 2) * 4 + y, (x % 2) * 8 + z * 2 + core)
 
@@ -92,7 +121,7 @@
     emb, ups,
     xbuf, ubuf, mbuf, gbuf, fin, st_src, st_dst,
     wqkv, wo, wd, wg, wu,
-    acts, part, rs_a, rs_b, rs_c, rs_d,
+    packs, acts, part, rs_a, rs_b, rs_c, rs_d,
     qkv_own, qkv_send, qkv_recv, qb, kb, vb, probs, ctx, dctx_own, dctx_send, dctx_recv, dqkv,
     ffn_own, ffn_send, ffn_recv, up_acc, ggu,
     ex_s, ex_r, st_s, st_r, x_s, x_r, y_s, y_r, ag_s, ag_r, rs_s, rs_r, cx_s, cx_r,
@@ -290,8 +319,11 @@
         return remote(ref, ref, ag_s.at[k, n_send], ag_r.at[k, n_recv], device)
 
     def ag_refs(k, index):
-        full = acts.at[k, index]
-        return full, acts.at[k, index, :, pl.ds(0, QUART)], acts.at[k, index, :, pl.ds(QUART, QUART)]
+        full = packs.at[k, index]
+        return full, packs.at[k, index, :, pl.ds(0, PHALF)], packs.at[k, index, :, pl.ds(PHALF, PHALF)]
+
+    def dense(k, index):
+        acts[DENSE[k], index] = unpack(packs[k, index]).astype(BF16)
 
     offs = (0, 3, 1, 2)
 
@@ -356,10 +388,17 @@
         for j in (1, 2, 3):
             through(j)
             yield
+
+        def near(n, carry):
+            dense(k, axes.slot(n % 4, n // 4 + n // 8))
+            return carry
+
+        lax.fori_loop(0, 12, near, 0)
         for j in range(4):
             far = ag_refs(k, axes.slot(offs[j], 2))
             arrived(far[1], ag_r.at[k, 6 + 4 * j])
             arrived(far[2], ag_r.at[k, 7 + 4 * j])
+            dense(k, axes.slot(offs[j], 2))
             pump(f"ag{k}.f{j}")
             yield
         for name in ("a", "b", "c", "d"):
@@ -378,7 +417,7 @@
             copy.start()
             return copy
 
-        lo, hi = pl.ds(0, QUART), pl.ds(QUART, QUART)
+        lo, hi = pl.ds(0, PHALF), pl.ds(PHALF, PHALF)
         sent = []
         compute(2)
         for i in (2, 1, 3, 0):
@@ -428,7 +467,7 @@
         total = total + rs_d[k, 0].astype(F32) + rs_d[k, 1].astype(F32)
         for copy in sent:
             copy.wait_send()
-        return total
+        return unpack(total)
 
     def both_halves(i, value):
         mine = jnp.broadcast_to(jnp.sum(value, axis=-1, keepdims=True), (ROWS, HD))
@@ -446,13 +485,13 @@
 
     def halves_matmul(op, k, weights_fn, send_ref, recv_ref, own_ref):
         def theirs(i, carry):
-            rows = acts[k, pl.ds(8 * other + 4 * i, 4)].reshape(GROUP, HALF)
+            rows = acts[DENSE[k], quad(other, i)].reshape(GROUP, HALF)
             send_ref[i] = weights_fn(rows).astype(BF16)
             swap_rows(op, i, send_ref.at[i], recv_ref.at[i]).start()
             return carry
 
         def ours(i, carry):
-            rows = acts[k, pl.ds(8 * core + 4 * i, 4)].reshape(GROUP, HALF)
+            rows = acts[DENSE[k], quad(core, i)].reshape(GROUP, HALF)
             own_ref[i] = weights_fn(rows)
             return carry
 
@@ -491,11 +530,11 @@
     ex[0].wait()
     inputs = xbuf[...]
     r_attn = lax.rsqrt(both_halves(0, inputs * inputs) + 1e-05)
-    acts[0, me] = (inputs * r_attn * gain_attn).astype(BF16)
+    packs[0, me] = pack(inputs * r_attn * gain_attn)
     along = Axes(1)
     ag_start(0, along)
     ex[1].wait()
-    acts[1, me] = ubuf[...].astype(BF16)
+    packs[1, me] = pack(ubuf[...])
     ag_first(1, along)
     pump("norm")
     ag_next(0, along)
@@ -539,14 +578,18 @@
     rows_wait(5, ctx)
 
     def spread_group(at, term):
-        def step(n, carry):
-            cols = pl.ds(pl.multiple_of(n * 512, 512), 512)
-            value = term(cols).astype(BF16)
+        def step(m, carry):
+            low = term(pl.ds(pl.multiple_of(m * 512, 512), 512))
+            high = term(pl.ds(pl.multiple_of(QUART + m * 512, 512), 512))
             for i in range(4):
-                part[mixed.slot(i, at), :, cols] = value[i * ROWS:(i + 1) * ROWS]
+                here = slice(i * ROWS, (i + 1) * ROWS)
+                index = mixed.slot(i, at)
+                for t, (upper, lower) in enumerate(zip(squeeze(low[here]), squeeze(high[here]))):
+                    cols = pl.ds(pl.multiple_of(t * QUART + m * 512, 512), 512)
+                    part[index, :, cols] = jnp.concatenate([upper, lower], axis=0).astype(BF16)
             return carry
 
-        lax.fori_loop(0, 4, step, 0)
+        lax.fori_loop(0, 2, step, 0)
 
     def out_term(at):
         rows = group_rows(ctx, at)
@@ -556,7 +599,7 @@
     mbuf[...] = middle
     pump("rs0")
     r_ffn = lax.rsqrt(both_halves(1, middle * middle) + 1e-05)
-    acts[2, me] = (middle * r_ffn * gain_ffn).astype(BF16)
+    packs[2, me] = pack(middle * r_ffn * gain_ffn)
     ag_start(2, mixed)
     pump("mid")
     ag_next(2, mixed)
@@ -576,7 +619,7 @@
     pump("gate")
     def up_depth(who, i, step):
         depth = pl.ds(pl.multiple_of(((y + step) % 4) * 512, 512), 512)
-        return dot_nn(acts[2, quad(who, i), :, depth].reshape(GROUP, 512), wu[depth])
+        return dot_nn(acts[DENSE[2], quad(who, i), :, depth].reshape(GROUP, 512), wu[depth])
 
     def up_first(i, carry):
         up_acc[i] = up_depth(other, i, 0) + up_depth(other, i, 1) + up_depth(other, i, 3)
@@ -631,7 +674,7 @@
     mean = both_halves(2, scaled * middle)
     grad_mid = ubuf[...] + r_ffn * scaled - middle * r_ffn**3 * mean
     gbuf[...] = grad_mid
-    acts[3, me] = grad_mid.astype(BF16)
+    packs[3, me] = pack(grad_mid)
     ag_start(3, mixed)
     ag_next(3, mixed)
     ag_rest(3, mixed)
@@ -724,9 +767,9 @@
             scratch(CROWS, D, dtype=F32),
             *[scratch(4, ROWS, HD, dtype=F32)] * 2,
             scratch(HALF, 512), scratch(256, HALF), scratch(FFB, HALF), scratch(HALF, FFB), scratch(HALF, FFB),
-            scratch(4, 16, ROWS, HALF), scratch(16, ROWS, HALF),
-            scratch(3, 2, 4, ROWS, QUART), scratch(3, 2, 4, ROWS, HALF),
-            scratch(3, 2, ROWS, QUART), scratch(3, 2, ROWS, HALF),
+            scratch(4, 16, 16, PACK), scratch(2, 16, ROWS, HALF), scratch(16, 16, PACK),
+            scratch(3, 2, 4, 16, PHALF), scratch(3, 2, 4, 16, PACK),
+            scratch(3, 2, 16, PHALF), scratch(3, 2, 16, PACK),
             scratch(2, GROUP, 512, dtype=F32), scratch(2, GROUP, 512), scratch(2, GROUP, 512),
             scratch(2, GROUP, 256), scratch(2, GROUP, HD), scratch(2, GROUP, HD),
             scratch(2, 2, GROUP, GROUP, dtype=F32), scratch(16, ROWS, 256),

time: 217 us -> 210 us (0.968)
  Pallas kernels: 214 us -> 207 us
    pallas_call x1, Pallas kernels: 214 us -> 207 us  [per_device(): pl.pallas_call(kernel, out_shape=jax.ShapeDtypeStruct((CROWS, D), F32), i...]
where the time goes in v4:
time: 210 us
  Pallas kernels  207 us (99%)
    pallas_call x1, Pallas kernels, per_device(): pl.pallas_call(kernel, out_shape=jax.ShapeDtypeStruct((CROWS, D), F32), i...  207 us

profile of v4, /device:TPU:1, one launch (start us, length us, event | category | flops | bytes accessed | tf_op | source)
XLA Modules:
  0.0 209.9 jit_solution(4678874843246469186)
XLA Ops:
  0.0 0.0 copy-start
  0.0 0.7 copy-done
  0.7 207.4 %shard_map.136 = f32[24,4096]{1,0:T(8,128)} custom-call(bf16[20,4096]{1,0:T(8,128)(2,1)} %emb_in.1, bf16[20,4096]{1,0:T(8,128)(2,1)} %ups_in.1, f32[1,4096]{1,0:T(1,128)} %bitcast.2, f32[1,4096]{1,0:T(1,128)} %bitcast.3, f32[192,128]{1,0:T(8,128)} %constant.6.clone.cos_ref, f32[192,128]{1,0:T(8,128)} %constant.7.clone.sin_ref, ...), custom_call_target="tpu_custom_call" | custom-call | flops 19000000512 | bytes 8000000 | tf_op jit(solution)/shard_map/pallas_call | solution.py:759
  208.1 1.8 multiply_convert_fusion
  (1 shorter events, 0.0 us)
Async XLA Ops:
  0.0 0.7 copy-start

commit v5 on v4

--- a/solution.py
+++ b/solution.py
@@ -35,7 +35,8 @@
             i, n = i if isinstance(i, tuple) else (i, 0)
             table.setdefault(point, []).append((what, who, i, n))
 
-    put("start", "y1", "diag", 1, 0, 2)
+    put("start", "y1", "diag", 1)
+    put("exchange", "y1", "diag", 0, 2)
     for i in (2, 3, 4):
         put("ups", "swap", "off", *((i, n) for n in range(CUTS)))
     put("ag0.t0", "y1", "off", 0, 1)
@@ -115,9 +116,10 @@
 
 
 def kernel(
-    emb_in, ups_in, gain_a, gain_f, cos_ref, sin_ref, mask_ref,
+    emb_hbm, ups_hbm, gain_a_hbm, gain_f_hbm, cos_hbm, sin_hbm, mask_hbm,
     w_q, w_kv, w_o, w_g, w_u, w_d,
     out_ref,
+    emb_in, ups_in, gain_a, gain_f, cos_ref, sin_ref, mask_ref, in_s,
     emb, ups,
     xbuf, ubuf, mbuf, gbuf, fin, st_src, st_dst,
     wqkv, wo, wd, wg, wu,
@@ -160,20 +162,20 @@
     col1 = pl.multiple_of(other * HALF, HALF)
     row0 = pl.multiple_of(core * CROWS, CROWS)
 
+    loads = [
+        pltpu.make_async_copy(src, dst, in_s.at[i])
+        for i, (src, dst) in enumerate((
+            (emb_hbm, emb_in), (ups_hbm, ups_in), (gain_a_hbm, gain_a), (gain_f_hbm, gain_f),
+            (cos_hbm, cos_ref), (sin_hbm, sin_ref), (mask_hbm, mask_ref),
+        ))
+    ]
+    for load in loads:
+        load.start()
     barrier = pltpu.get_barrier_semaphore()
     friends = (partner, across_same, across_other, y_up, y_dn, x_up, x_dn, z_up, z_dn)
     for friend in friends:
         pl.semaphore_signal(barrier, inc=1, device_id=friend, device_id_type=MESH)
-    for wide, given in ((emb, emb_in), (ups, ups_in)):
-        wide[pl.ds(LIVE // 8 * 8, 8)] = jnp.zeros((8, D), F32)
-        wide[pl.ds(0, LIVE)] = given[...].astype(F32)
     pl.semaphore_wait(barrier, len(friends))
-
-    ex = []
-    for i, (src, dst) in enumerate(((emb, xbuf), (ups, ubuf))):
-        copy = remote(src.at[:, pl.ds(col1, HALF)], dst.at[pl.ds(row0, CROWS)], ex_s.at[i], ex_r.at[i], partner)
-        copy.start()
-        ex.append(copy)
 
     yrow = pl.multiple_of(y * 512, 512)
     kvcol = pl.multiple_of(256 + core * HD, HD)
@@ -523,6 +525,18 @@
     for i in range(5):
         swap_local(i)
     pump("start")
+
+    for load in loads:
+        load.wait()
+    for wide, given in ((emb, emb_in), (ups, ups_in)):
+        wide[pl.ds(LIVE // 8 * 8, 8)] = jnp.zeros((8, D), F32)
+        wide[pl.ds(0, LIVE)] = given[...].astype(F32)
+    ex = []
+    for i, (src, dst) in enumerate(((emb, xbuf), (ups, ubuf))):
+        copy = remote(src.at[:, pl.ds(col1, HALF)], dst.at[pl.ds(row0, CROWS)], ex_s.at[i], ex_r.at[i], partner)
+        copy.start()
+        ex.append(copy)
+    pump("exchange")
     gain_attn = gain_a[:, pl.ds(col0, HALF)]
     gain_ffn = gain_f[:, pl.ds(col0, HALF)]
     xbuf[pl.ds(row0, CROWS)] = emb[:, pl.ds(col0, HALF)]
@@ -759,9 +773,11 @@
     result = pl.pallas_call(
         kernel,
         out_shape=jax.ShapeDtypeStruct((CROWS, D), F32),
-        in_specs=[vmem] * 7 + [hbm] * 6,
+        in_specs=[hbm] * 13,
         out_specs=vmem,
         scratch_shapes=[
+            *[scratch(LIVE, D)] * 2, *[scratch(1, D, dtype=F32)] * 2,
+            *[scratch(GROUP, HD, dtype=F32)] * 2, scratch(GROUP, GROUP, dtype=F32), dma((7,)),
             *[scratch(CROWS, D, dtype=F32)] * 2,
             *[scratch(ROWS, HALF, dtype=F32)] * 4,
             scratch(CROWS, D, dtype=F32),

time: 210 us -> 209 us (level)
  no operation moved by 1% of the time
where the time goes in v5:
time: 209 us
  Pallas kernels  206 us (99%)
    pallas_call x1, Pallas kernels, per_device(): pl.pallas_call(kernel, out_shape=jax.ShapeDtypeStruct((CROWS, D), F32), i...  206 us

profile of v5, /device:TPU:1, one launch (start us, length us, event | category | flops | bytes accessed | tf_op | source)
XLA Modules:
  0.0 208.7 jit_solution(14878648673557825882)
XLA Ops:
  0.0 0.0 copy-start
  0.0 0.7 copy-done
  0.7 206.3 %shard_map.136 = f32[24,4096]{1,0:T(8,128)} custom-call(bf16[20,4096]{1,0:T(8,128)(2,1)} %emb_hbm.1, bf16[20,4096]{1,0:T(8,128)(2,1)} %ups_hbm.1, f32[1,4096]{1,0:T(1,128)} %bitcast.2, f32[1,4096]{1,0:T(1,128)} %bitcast.3, f32[192,128]{1,0:T(8,128)} %constant.6.clone.cos_hbm, f32[192,128]{1,0:T(8,128)} %constant.7.clone.sin_hbm, ...), custom_call_target="tpu_custom_call" | custom-call | flops 19000000512 | bytes 8000000 | tf_op jit(solution)/shard_map/pallas_call | solution.py:773
  207.0 1.8 multiply_convert_fusion
  (1 shorter events, 0.0 us)
Async XLA Ops:
  0.0 0.7 copy-start

commit v6 on v5

--- a/solution.py
+++ b/solution.py
@@ -421,14 +421,13 @@
 
         lo, hi = pl.ds(0, PHALF), pl.ds(PHALF, PHALF)
         sent = []
-        compute(2)
+        compute((2,))
         for i in (2, 1, 3, 0):
             at = mixed.slot(i, 2)
             sent.append(send(part.at[at, :, lo], rs_a.at[k, 0, i], 2 * i, mixed.r2_up))
             sent.append(send(part.at[at, :, hi], rs_a.at[k, 1, i], 2 * i + 1, mixed.r2_dn))
         pump(f"rs{k}.0")
-        compute(1)
-        compute(3)
+        compute((1, 3))
         for i in (2, 1, 3, 0):
             at = mixed.slot(i, 1)
             arrived(rs_a.at[k, 0, i], rs_r.at[k, 2 * i])
@@ -439,7 +438,7 @@
             part[at, :, hi] = (part[at, :, hi].astype(F32) + rs_a[k, 1, i].astype(F32)).astype(BF16)
             sent.append(send(part.at[at], rs_b.at[k, 1, i], 9 + 2 * i, mixed.r2_dn))
             pump(f"rs{k}.t{i}")
-        compute(0)
+        compute((0,))
         pump(f"rs{k}.1")
 
         def add_both(i):
@@ -479,8 +478,8 @@
         copy.wait()
         return (mine + st_dst[i])[:, :1] * (1.0 / D)
 
-    def group_rows(ref, at):
-        return jnp.concatenate([ref[mixed.slot(i, at)] for i in range(4)], axis=0)
+    def group_rows(ref, ats):
+        return jnp.concatenate([ref[mixed.slot(i, at)] for at in ats for i in range(4)], axis=0)
 
     def swap_rows(op, i, src, dst):
         return remote(src, dst, cx_s.at[2 * op + i], cx_r.at[2 * op + i], partner)
@@ -591,13 +590,13 @@
     y_finish(1)
     rows_wait(5, ctx)
 
-    def spread_group(at, term):
+    def spread_group(ats, term):
         def step(m, carry):
             low = term(pl.ds(pl.multiple_of(m * 512, 512), 512))
             high = term(pl.ds(pl.multiple_of(QUART + m * 512, 512), 512))
-            for i in range(4):
+            for i in range(4 * len(ats)):
                 here = slice(i * ROWS, (i + 1) * ROWS)
-                index = mixed.slot(i, at)
+                index = mixed.slot(i % 4, ats[i // 4])
                 for t, (upper, lower) in enumerate(zip(squeeze(low[here]), squeeze(high[here]))):
                     cols = pl.ds(pl.multiple_of(t * QUART + m * 512, 512), 512)
                     part[index, :, cols] = jnp.concatenate([upper, lower], axis=0).astype(BF16)

time: 209 us -> 207 us (level)
  no operation moved by 1% of the time
where the time goes in v6:
time: 207 us
  Pallas kernels  205 us (99%)
    pallas_call x1, Pallas kernels, per_device(): pl.pallas_call(kernel, out_shape=jax.ShapeDtypeStruct((CROWS, D), F32), i...  205 us

profile of v6, /device:TPU:1, one launch (start us, length us, event | category | flops | bytes accessed | tf_op | source)
XLA Modules:
  0.0 207.3 jit_solution(13167336933029835298)
XLA Ops:
  0.0 0.0 copy-start
  0.0 0.7 copy-done
  0.7 204.9 %shard_map.136 = f32[24,4096]{1,0:T(8,128)} custom-call(bf16[20,4096]{1,0:T(8,128)(2,1)} %emb_hbm.1, bf16[20,4096]{1,0:T(8,128)(2,1)} %ups_hbm.1, f32[1,4096]{1,0:T(1,128)} %bitcast.2, f32[1,4096]{1,0:T(1,128)} %bitcast.3, f32[192,128]{1,0:T(8,128)} %constant.6.clone.cos_hbm, f32[192,128]{1,0:T(8,128)} %constant.7.clone.sin_hbm, ...), custom_call_target="tpu_custom_call" | custom-call | flops 19000000512 | bytes 8000000 | tf_op jit(solution)/shard_map/pallas_call | solution.py:772
  205.5 1.8 multiply_convert_fusion
  (1 shorter events, 0.0 us)
Async XLA Ops:
  0.0 0.7 copy-start

commit v7 on v6

--- a/solution.py
+++ b/solution.py
@@ -496,6 +496,15 @@
             own_ref[i] = weights_fn(rows)
             return carry
 
+        if op == 4:
+            value = weights_fn(acts[DENSE[k], pl.ds(8 * other, 8)].reshape(2 * GROUP, HALF)).astype(BF16)
+            for i in range(2):
+                send_ref[i] = value[i * GROUP:(i + 1) * GROUP]
+                swap_rows(op, i, send_ref.at[i], recv_ref.at[i]).start()
+            value = weights_fn(acts[DENSE[k], pl.ds(8 * core, 8)].reshape(2 * GROUP, HALF))
+            for i in range(2):
+                own_ref[i] = value[i * GROUP:(i + 1) * GROUP]
+            return
         lax.fori_loop(0, 2, theirs, 0)
         lax.fori_loop(0, 2, ours, 0)
 

time: 207 us -> 208 us (level)
  no operation moved by 1% of the time
where the time goes in v7:
time: 208 us; the launch traced here: 207 us
  Pallas kernels  205 us (99%)
    pallas_call x1, Pallas kernels, per_device(): pl.pallas_call(kernel, out_shape=jax.ShapeDtypeStruct((CROWS, D), F32), i...  205 us

profile of v7, /device:TPU:1, one launch (start us, length us, event | category | flops | bytes accessed | tf_op | source)
XLA Modules:
  0.0 207.4 jit_solution(3085932795664646625)
XLA Ops:
  0.0 0.0 copy-start
  0.0 0.7 copy-done
  0.7 204.9 %shard_map.136 = f32[24,4096]{1,0:T(8,128)} custom-call(bf16[20,4096]{1,0:T(8,128)(2,1)} %emb_hbm.1, bf16[20,4096]{1,0:T(8,128)(2,1)} %ups_hbm.1, f32[1,4096]{1,0:T(1,128)} %bitcast.2, f32[1,4096]{1,0:T(1,128)} %bitcast.3, f32[192,128]{1,0:T(8,128)} %constant.6.clone.cos_hbm, f32[192,128]{1,0:T(8,128)} %constant.7.clone.sin_hbm, ...), custom_call_target="tpu_custom_call" | custom-call | flops 19000000512 | bytes 8000000 | tf_op jit(solution)/shard_map/pallas_call | solution.py:781
  205.6 1.8 multiply_convert_fusion
  (1 shorter events, 0.0 us)
Async XLA Ops:
  0.0 0.7 copy-start
